TPU v7x, 256 devices: a whole 4x4x8 slice. The times are simulated.
256 devices in a mesh: dp: 4 (over x_lo, core), blk: 64 (over z, y, x_hi).
Axes of the slice: x: 4 (x_hi: 2, x_lo: 2; x = x_hi * 2 + x_lo), y: 4, z: 8, core: 2. Of those that a mesh axis runs over, the one named last changes fastest.
Arguments:
- visual_features: bfloat16 [163840, 1152], P(('dp', 'blk')), parts along dimension 0, may hold values from -6 to 6
- caption_features: bfloat16 [163840, 1152], P(('dp', 'blk')), parts along dimension 0, may hold values from -6 to 6
- sharpness_scale: float32 [1], replicated, may hold values from 20 to 60
- score_shift: float32 [1], replicated, may hold values from -4 to -1
Outputs:
- image_grad: float32 [163840, 1152], P(('dp', 'blk')), parts along dimension 0
- text_grad: float32 [163840, 1152], P(('dp', 'blk')), parts along dimension 0
There are 4 independent parts, one for each index of `dp`. A program takes and returns all parts, laid end to end along the dimension named above; an argument that names none is the same for every part. Nothing has to cross between parts.
All inputs are finite; a program needn't handle non-finite values.
Results may differ from a plain program's by a relative error of at most 0.0065.
Values may be sent and summed in bfloat16 or wider, within the bound.
No kernel may reach another device: no remote copies, remote signals or barrier semaphores. Data moves between devices by JAX's collectives and lax.ppermute only.
A program may use at most 64 MiB of HBM per device.

v0:
```python
import functools

import jax
import jax.numpy as jnp
from jax import lax
from jax.experimental import pallas as pl
from jax.experimental.pallas import tpu as pltpu
from jax.sharding import PartitionSpec as P

EPSILON = 1e-06
LOG2_E = 1.4426950408889634
FIRST = (256, 256, 128)
SECOND = (256, 256, 128)
PLAN = (
    ("go", "r10", "s20", "r11", "s10", "s21"),
    ("first",),
    ("wait", "r10", "s20", "k1"),
    ("go", "r20", "s22"),
    ("wait", "r11", "s21"),
    ("go", "r21", "q10"),
    ("wait", "s10", "s22"),
    ("go", "q11"),
    ("add1", "s20", "s21", "s22", "r10", "r11"),
    ("wait", "r20", "k1"),
    ("go", "q20", "r12"),
    ("add2", "s10", "r20"),
    ("wait", "r21", "q10", "k2"),
    ("go", "q21", "r22"),
    ("add2", "r21", "q20"),
    ("wait", "r12", "k2"),
    ("go", "q12"),
    ("add1", "q10", "q11", "r12"),
    ("wait", "r22", "k1"),
    ("go", "q22"),
    ("end1", "q12"),
    ("add2", "r22", "q21"),
    ("end2", "q22"),
)
TILE = 320


def normalized(rows):
    values = rows.astype(jnp.float32)
    inverse = 1.0 / jnp.sqrt(jnp.sum(values * values, axis=1, keepdims=True) + EPSILON)
    return values * inverse, inverse


def slopes_of(scalars, own, partners, first_row=None):
    products = lax.dot_general(
        own, partners, (((1,), (1,)), ((), ())), preferred_element_type=jnp.float32
    )
    exponents = products * (-LOG2_E * scalars[0]) - LOG2_E * scalars[1]
    if first_row is not None:
        rows = lax.broadcasted_iota(jnp.int32, products.shape, 0) + first_row
        same = rows == lax.broadcasted_iota(jnp.int32, products.shape, 1)
        exponents = jnp.where(same, -exponents, exponents)
    slopes = 1.0 / (1.0 + jnp.exp2(exponents))
    if first_row is not None:
        slopes = jnp.where(same, -slopes, slopes)
    return slopes.astype(jnp.bfloat16)


def against(scalars, own, partners):
    return jnp.dot(
        slopes_of(scalars, own, partners), partners, preferred_element_type=jnp.float32
    )


def tiles(rows):
    return [pl.ds(a, TILE) for a in range(0, rows, TILE)]


def fill(units, partners):
    at = 0
    for partner in partners:
        for a in range(0, partner.shape[0], 128):
            n = min(128, partner.shape[0] - a)
            units[at + a : at + a + n, :] = normalized(partner[a : a + n, :])[0].astype(
                jnp.bfloat16
            )
        at += partner.shape[0]


def first_kernel(scalars, own1, own2, unit1, unit2, sums1, sums2, slopes):
    fill(unit1, [own1])
    fill(unit2, [own2])
    for a in range(0, own1.shape[0], TILE):
        rows = pl.ds(a, TILE)
        slopes[rows, :] = slopes_of(scalars, unit1[rows, :], unit2[...], a)
        sums1[rows, :] = jnp.dot(
            slopes[rows, :], unit2[...], preferred_element_type=jnp.float32
        )
    sums2[...] = lax.dot_general(
        slopes[...], unit1[...], (((0,), (0,)), ((), ())), preferred_element_type=jnp.float32
    )


def middle_kernel(n, scalars, unit, old, *refs):
    sums, scratch = refs[n:]
    fill(scratch, refs[:n])
    for rows in tiles(unit.shape[0]):
        sums[rows, :] = old[rows, :] + against(scalars, unit[rows, :], scratch[...])


def project(scalars, own, sums, first, outs, semaphores):
    rows = own.shape[0]
    step = 128
    for a in range(0, rows, step):
        piece = pl.ds(a, step)
        units, inverse = normalized(own[piece, :])
        gradient = scalars[0] * sums[piece, :]
        along = jnp.sum(units * gradient, axis=1, keepdims=True)
        sums[piece, :] = (gradient - units * along) * inverse

        def copy(which):
            return pltpu.make_async_copy(
                sums.at[piece, :], outs[which].at[piece, :], semaphores.at[a // step]
            )

        @pl.when(first)
        def _():
            copy(0).start()

        @pl.when(jnp.logical_not(first))
        def _():
            copy(1).start()

    for a in range(0, rows, step):
        piece = pl.ds(a, step)
        pltpu.make_async_copy(
            sums.at[piece, :], outs[0].at[piece, :], semaphores.at[a // step]
        ).wait()


def last_kernel(n, side, scalars, own, unit, old, *refs):
    out0, out1, scratch, total, semaphores = refs[-5:]
    fill(scratch, refs[:n])
    for rows in tiles(unit.shape[0]):
        total[rows, :] = old[rows, :] + against(scalars, unit[rows, :], scratch[...])
    first = scalars[2] > 0.5 if side == 1 else scalars[2] < 0.5
    project(scalars, own, total, first, (out0, out1), semaphores)


VMEM = pl.BlockSpec(memory_space=pltpu.VMEM)
SMEM = pl.BlockSpec(memory_space=pltpu.SMEM)
HBM = pl.BlockSpec(memory_space=pl.ANY)


def call(kernel, operands, specs, out_shape, out_specs, scratch, pairs, aliases=None):
    width = operands[1].shape[1]
    return pl.pallas_call(
        kernel,
        in_specs=specs,
        out_specs=out_specs,
        out_shape=out_shape,
        scratch_shapes=scratch,
        input_output_aliases=aliases or {},
        cost_estimate=pl.CostEstimate(
            flops=4 * pairs * width, bytes_accessed=1 << 20, transcendentals=2 * pairs
        ),
        compiler_params=pltpu.CompilerParams(vmem_limit_bytes=20 * 1024 * 1024),
    )(*operands)


def shards(visual, caption, sharpness_scale, score_shift):
    blocks = lax.axis_size("blk")
    cells = blocks // 2
    even = lax.axis_index("blk") % 2 == 0
    rows, width = visual.shape

    def at(cell, half):
        return 2 * (cell % cells) + half

    cross = [(b, b ^ 1) for b in range(blocks)]
    outward = [(at(c, h), at(c + 1 - 2 * h, h)) for c in range(cells) for h in (0, 1)]
    inward = [(at(c, h), at(c - 1 + 2 * h, h)) for c in range(cells) for h in (0, 1)]

    def one(a, b):
        return jnp.where(even, caption[a:b], visual[a:b])

    def two(a, b):
        return jnp.where(even, visual[a:b], caption[a:b])

    def spans(sizes):
        ends = [sum(sizes[:k]) for k in range(len(sizes) + 1)]
        return list(zip(ends, ends[1:]))

    heads = one(0, FIRST[0]), two(0, SECOND[0])
    caption, visual = lax.optimization_barrier((caption, visual, heads))[:2]
    own1, own2 = one(0, rows), two(0, rows)
    flag = jnp.where(even, 0.0, 1.0)
    scalars = jnp.stack([sharpness_scale[0], score_shift[0], flag])

    real = jax.ShapeDtypeStruct((rows, width), jnp.float32)
    half = jax.ShapeDtypeStruct((rows, width), jnp.bfloat16)

    def count(partners):
        return sum(p.shape[0] for p in partners)

    def units_of(partners):
        return pltpu.VMEM((max(count(partners), 16), width), jnp.bfloat16)

    def middle(unit, sums, partners):
        operands = [scalars, unit, sums, *partners]
        return call(
            functools.partial(middle_kernel, len(partners)),
            operands,
            [SMEM] + [VMEM] * (len(operands) - 1),
            real,
            VMEM,
            [units_of(partners)],
            rows * count(partners),
            {2: 0},
        )

    def last(side, own, unit, sums, partners, outs):
        operands = [scalars, own, unit, sums, *partners, *outs]
        n = len(operands)
        return call(
            functools.partial(last_kernel, len(partners), side),
            operands,
            [SMEM] + [VMEM] * (n - 1 - len(outs)) + [HBM] * len(outs),
            (real, real),
            (HBM, HBM),
            [units_of(partners), *staging],
            rows * count(partners),
            {n - 2: 0, n - 1: 1} if outs else {},
        )

    staging = [
        pltpu.VMEM((rows, width), jnp.float32),
        pltpu.SemaphoreType.DMA((rows // 128,)),
    ]

    there, ready = {}, {}
    for k, (a, b) in enumerate(spans(FIRST)):
        ready["r1", k] = functools.partial(one, a, b)
        ready["q1", k] = functools.partial(there.get, ("r1", k))
    for k, (a, b) in enumerate(spans(SECOND)):
        ready["s2", k] = functools.partial(two, a, b)
        ready["r2", k] = functools.partial(there.get, ("s2", k))
        ready["q2", k] = functools.partial(there.get, ("r2", k))
    ready["r1", 0], ready["s2", 0] = lambda: heads[0], lambda: heads[1]
    ready["s1", 0] = lambda: own1
    routes = {"r1": cross, "q1": inward, "s1": outward, "s2": inward, "r2": cross, "q2": outward}

    done, outs = (), ()
    sums, units = {}, {}
    for action, *names in PLAN:
        names = [(n[:2], int(n[2:] or 0)) for n in names]
        if action == "wait":
            done = tuple(there[n] if n in there else sums[int(n[0][1])] for n in names)
        elif action == "go":
            values = tuple(ready[n]() for n in names)
            if done:
                values = lax.optimization_barrier((values, done))[0]
            for n, value in zip(names, values):
                there[n] = lax.ppermute(value, "blk", routes[n[0]])
        elif action == "first":
            units[1], units[2], sums[1], sums[2] = call(
                first_kernel,
                [scalars, own1, own2],
                [SMEM, VMEM, VMEM],
                (half, half, real, real),
                (VMEM,) * 4,
                [pltpu.VMEM((rows, rows), jnp.bfloat16)],
                2 * rows * rows,
            )
        else:
            side = int(action[-1])
            partners = [there[n] for n in names]
            if action[:-1] == "add":
                sums[side] = middle(units[side], sums[side], partners)
            else:
                outs = last(side, (own1, own2)[side - 1], units[side], sums[side], partners, outs)
    return outs


def solution(mesh):
    placed = (P(("dp", "blk"), None), P(("dp", "blk"), None), P(), P())
    return jax.shard_map(
        shards,
        mesh=mesh,
        in_specs=placed,
        out_specs=(P(("dp", "blk"), None), P(("dp", "blk"), None)),
        check_vma=False,
    )
```

profile of v0, /device:TPU:2, one launch (start us, length us, event | category | flops | bytes accessed | tf_op | source)
XLA Modules:
  0.0 97.1 jit_solution(487119979958126419)
XLA Ops:
  0.6 0.0 copy-start
  0.7 2.5 %broadcast_select_fusion.4 = (bf16[256,1152]{1,0:T(8,128)(2,1)}, bf16[256,1152]{1,0:T(8,128)(2,1)}) fusion(pred[]{:T(512)S(6)} %eq.5, bf16[640,1152]{1,0:T(8,128)(2,1)} %param.4, bf16[640,1152]{1,0:T(8,128)(2,1)} %param.5), kind=kLoop, calls=%fused_computation.4 | loop fusion | flops 589824 | bytes 2359297 | tf_op jit(solution)/shard_map/jit(_where)/select_n | solution.py:182
  3.1 2.1 %collective-permute-start.2 = (bf16[256,1152]{1,0:T(8,128)(2,1)}, bf16[256,1152]{1,0:T(8,128)(2,1)}, u32[]{:S(2)}, u32[]{:S(2)}) collective-permute-start(bf16[256,1152]{1,0:T(8,128)(2,1)} %get-tuple-element.47), channel_id=1, source_target_pairs={{0,1},{1,0},{2,3},{3,2},{4,5},{5,4},{6,7},{7,6},{8,9},{9,8},{10,11... | collective-permute-start | bytes 1769480 | tf_op jit(solution)/shard_map/ppermute | solution.py:258
  5.3 8.3 %collective-permute-start.1 = (bf16[256,1152]{1,0:T(8,128)(2,1)}, bf16[256,1152]{1,0:T(8,128)(2,1)}, u32[]{:S(2)}, u32[]{:S(2)}) collective-permute-start(bf16[256,1152]{1,0:T(8,128)(2,1)} %get-tuple-element.46), channel_id=1, source_target_pairs={{0,62},{1,3},{2,0},{3,5},{4,2},{5,7},{6,4},{7,9},{8,6},{9,11},{10,... | collective-permute-start | bytes 1769480 | tf_op jit(solution)/shard_map/ppermute | solution.py:258
  13.6 0.0 copy-done
  13.6 1.7 %broadcast_select_fusion = (bf16[640,1152]{1,0:T(8,128)(2,1)S(1)}, bf16[640,1152]{1,0:T(8,128)(2,1)S(1)}) fusion(bf16[640,1152]{1,0:T(8,128)(2,1)S(1)} %copy-done, bf16[640,1152]{1,0:T(8,128)(2,1)} %param.4, pred[]{:T(512)S(6)} %eq.5), kind=kLoop, calls=%fused_computation | loop fusion | flops 1474560 | bytes 5898241 | tf_op jit(solution)/shard_map/jit(_where)/select_n | solution.py:179
  15.2 0.1 collective-permute-start
  15.3 0.0 copy-done.1
  15.3 1.1 %broadcast_select_fusion.2 = (bf16[256,1152]{1,0:T(8,128)(2,1)}, bf16[256,1152]{1,0:T(8,128)(2,1)}) fusion(pred[]{:T(512)S(6)} %eq.5, bf16[640,1152]{1,0:T(8,128)(2,1)S(1)} %copy-done, bf16[640,1152]{1,0:T(8,128)(2,1)S(1)} %copy-done.1), kind=kLoop, calls=%fused_computation.2 | loop fusion | flops 589824 | bytes 2359297 | tf_op jit(solution)/shard_map/jit(_where)/select_n | solution.py:179
  16.5 1.5 %collective-permute-start.5 = (bf16[256,1152]{1,0:T(8,128)(2,1)}, bf16[256,1152]{1,0:T(8,128)(2,1)S(1)}, u32[]{:S(2)}, u32[]{:S(2)}) collective-permute-start(bf16[256,1152]{1,0:T(8,128)(2,1)} %get-tuple-element.42), channel_id=1, source_target_pairs={{0,1},{1,0},{2,3},{3,2},{4,5},{5,4},{6,7},{7,6},{8,9},{9,8},{10,11... | collective-permute-start | bytes 1769480 | tf_op jit(solution)/shard_map/ppermute | solution.py:258
  18.0 3.8 %collective-permute-start.4 = (bf16[256,1152]{1,0:T(8,128)(2,1)}, bf16[256,1152]{1,0:T(8,128)(2,1)}, u32[]{:S(2)}, u32[]{:S(2)}) collective-permute-start(bf16[256,1152]{1,0:T(8,128)(2,1)} %get-tuple-element.43), channel_id=1, source_target_pairs={{0,62},{1,3},{2,0},{3,5},{4,2},{5,7},{6,4},{7,9},{8,6},{9,11},{10,... | collective-permute-start | bytes 1769480 | tf_op jit(solution)/shard_map/ppermute | solution.py:258
  21.8 0.9 broadcast_select_fusion.6
  24.0 0.1 pad_maximum_fusion.scalars
  24.1 5.6 %shard_map.59 = (bf16[640,1152]{1,0:T(8,128)(2,1)S(1)}, bf16[640,1152]{1,0:T(8,128)(2,1)S(1)}, f32[640,1152]{1,0:T(8,128)S(1)}, f32[640,1152]{1,0:T(8,128)S(1)}) custom-call(f32[3]{0:T(128)S(1)} %pad_maximum_fusion.scalars, bf16[640,1152]{1,0:T(8,128)(2,1)S(1)} %get-tuple-element.44.own1.own, bf16[640,1152]{1,0:T(8,128)(2,1)S(1)} %get-tuple-element.45.own2.own), custom_call_target="tpu_custom_call" | custom-call | flops 3774873600 | bytes 1048576 | tf_op jit(solution)/shard_map/pallas_call | solution.py:151
  29.6 0.0 collective-permute-done.2.refs_3_
  29.6 0.0 collective-permute-done.1.refs_0_
  29.7 3.8 %collective-permute-start.7 = (bf16[128,1152]{1,0:T(8,128)(2,1)S(1)}, bf16[128,1152]{1,0:T(8,128)(2,1)S(1)}, u32[]{:S(2)}, u32[]{:S(2)}) collective-permute-start(bf16[128,1152]{1,0:T(8,128)(2,1)S(1)} %copy-done.3), channel_id=1, source_target_pairs={{0,62},{1,3},{2,0},{3,5},{4,2},{5,7},{6,4},{7,9},{8,6},{9,11},{10,... | collective-permute-start | bytes 884744 | tf_op jit(solution)/shard_map/ppermute | solution.py:258
  33.5 0.0 collective-permute-start.3
  33.5 0.0 collective-permute-done.5.refs_4_
  33.5 6.8 %collective-permute-done.4.refs_1_ = bf16[256,1152]{1,0:T(8,128)(2,1)} collective-permute-done((bf16[256,1152]{1,0:T(8,128)(2,1)}, bf16[256,1152]{1,0:T(8,128)(2,1)}, u32[]{:S(2)}, u32[]{:S(2)}) %collective-permute-start.4) | collective-permute-done | bytes 589856 | tf_op jit(solution)/shard_map/ppermute | solution.py:258
  40.3 5.8 %collective-permute-start.9 = (bf16[256,1152]{1,0:T(8,128)(2,1)}, bf16[256,1152]{1,0:T(8,128)(2,1)S(1)}, u32[]{:S(2)}, u32[]{:S(2)}) collective-permute-start(bf16[256,1152]{1,0:T(8,128)(2,1)} %collective-permute-done.2.refs_3_), channel_id=1, source_target_pairs={{0,62},{1,3},{2,0},{3,5},{4,2},{5,7},{6,4},{7,9},{8,6},{9,11},{10,... | collective-permute-start | bytes 1769480 | tf_op jit(solution)/shard_map/ppermute | solution.py:258
  46.1 0.0 collective-permute-start.6
  46.1 0.3 collective-permute-done.7.refs_2_
  46.4 6.6 %shard_map.61.old = f32[640,1152]{1,0:T(8,128)S(1)} custom-call(f32[3]{0:T(128)S(1)} %pad_maximum_fusion.scalars, bf16[640,1152]{1,0:T(8,128)(2,1)S(1)} %get-tuple-element.28.unit, f32[640,1152]{1,0:T(8,128)S(1)} %get-tuple-element.25.old, bf16[256,1152]{1,0:T(8,128)(2,1)} %collective-permute-done.1.refs_0_, ...), custom_call_target="tpu_custom_call", output_to_operand_aliasing={{}: (2, {})} | custom-call | flops 3397386240 | bytes 1048576 | tf_op jit(solution)/shard_map/pallas_call | solution.py:151
  53.0 0.0 collective-permute-done.3.refs_1_
  53.0 0.1 collective-permute-start.8
  53.1 0.0 collective-permute-done.refs_0_
  53.1 5.9 %collective-permute-start.12 = (bf16[256,1152]{1,0:T(8,128)(2,1)S(1)}, bf16[256,1152]{1,0:T(8,128)(2,1)S(1)}, u32[]{:S(2)}, u32[]{:S(2)}) collective-permute-start(bf16[256,1152]{1,0:T(8,128)(2,1)S(1)} %collective-permute-done.5.refs_4_), channel_id=1, source_target_pairs={{0,62},{1,3},{2,0},{3,5},{4,2},{5,7},{6,4},{7,9},{8,6},{9,11},{10,... | collective-permute-start | bytes 1769480 | tf_op jit(solution)/shard_map/ppermute | solution.py:258
  59.0 0.0 collective-permute-start.13
  59.0 5.5 %shard_map.60.old = f32[640,1152]{1,0:T(8,128)S(1)} custom-call(f32[3]{0:T(128)S(1)} %pad_maximum_fusion.scalars, bf16[640,1152]{1,0:T(8,128)(2,1)S(1)} %get-tuple-element.23.unit, f32[640,1152]{1,0:T(8,128)S(1)} %get-tuple-element.24.old, bf16[640,1152]{1,0:T(8,128)(2,1)} %collective-permute-done.refs_0_, ...), custom_call_target="tpu_custom_call", output_to_operand_aliasing={{}: (2, {})} | custom-call | flops 2642411520 | bytes 1048576 | tf_op jit(solution)/shard_map/pallas_call | solution.py:151
  64.5 0.0 collective-permute-done.9.refs_0_
  64.5 0.0 collective-permute-done.6.refs_0_
  64.5 0.1 collective-permute-start.11
  64.6 5.4 %collective-permute-start.10 = (bf16[128,1152]{1,0:T(8,128)(2,1)S(1)}, bf16[128,1152]{1,0:T(8,128)(2,1)S(1)}, u32[]{:S(2)}, u32[]{:S(2)}) collective-permute-start(bf16[128,1152]{1,0:T(8,128)(2,1)S(1)} %collective-permute-done.7.refs_2_), channel_id=1, source_target_pairs={{0,1},{1,0},{2,3},{3,2},{4,5},{5,4},{6,7},{7,6},{8,9},{9,8},{10,11... | collective-permute-start | bytes 884744 | tf_op jit(solution)/shard_map/ppermute | solution.py:258
  70.1 1.6 %collective-permute-done.8.refs_1_ = bf16[256,1152]{1,0:T(8,128)(2,1)S(1)} collective-permute-done((bf16[256,1152]{1,0:T(8,128)(2,1)S(1)}, bf16[256,1152]{1,0:T(8,128)(2,1)S(1)}, u32[]{:S(2)}, u32[]{:S(2)}) %collective-permute-start.8) | collective-permute-done | bytes 589856 | tf_op jit(solution)/shard_map/ppermute | solution.py:258
  71.7 3.1 %shard_map.62.old = f32[640,1152]{1,0:T(8,128)S(1)} custom-call(f32[3]{0:T(128)S(1)} %pad_maximum_fusion.scalars, bf16[640,1152]{1,0:T(8,128)(2,1)S(1)} %get-tuple-element.23.unit, f32[640,1152]{1,0:T(8,128)S(1)} %shard_map.60.old, bf16[256,1152]{1,0:T(8,128)(2,1)S(1)} %collective-permute-done.6.refs_0_, ...), custom_call_target="tpu_custom_call", output_to_operand_aliasing={{}: (2, {})} | custom-call | flops 1509949440 | bytes 1048576 | tf_op jit(solution)/shard_map/pallas_call | solution.py:151
  74.8 0.0 collective-permute-done.13.refs_2_
  74.9 3.4 %collective-permute-start.15 = (bf16[128,1152]{1,0:T(8,128)(2,1)S(1)}, bf16[128,1152]{1,0:T(8,128)(2,1)S(1)}, u32[]{:S(2)}, u32[]{:S(2)}) collective-permute-start(bf16[128,1152]{1,0:T(8,128)(2,1)S(1)} %collective-permute-done.13.refs_2_), channel_id=1, source_target_pairs={{0,62},{1,3},{2,0},{3,5},{4,2},{5,7},{6,4},{7,9},{8,6},{9,11},{10,... | collective-permute-start | bytes 884744 | tf_op jit(solution)/shard_map/ppermute | solution.py:258
  78.2 0.0 collective-permute-done.12.refs_1_
  78.3 4.0 %shard_map.64.old = f32[640,1152]{1,0:T(8,128)S(1)} custom-call(f32[3]{0:T(128)S(1)} %pad_maximum_fusion.scalars, bf16[640,1152]{1,0:T(8,128)(2,1)S(1)} %get-tuple-element.28.unit, f32[640,1152]{1,0:T(8,128)S(1)} %shard_map.61.old, bf16[256,1152]{1,0:T(8,128)(2,1)S(1)} %collective-permute-done.9.refs_0_, ...), custom_call_target="tpu_custom_call", output_to_operand_aliasing={{}: (2, {})} | custom-call | flops 1887436800 | bytes 1048576 | tf_op jit(solution)/shard_map/pallas_call | solution.py:151
  82.3 0.0 collective-permute-done.10.refs_0_
  82.3 0.3 collective-permute-start.14
  82.7 0.0 collective-permute-done.15.refs_0_
  82.7 4.2 %shard_map.65 = (f32[640,1152]{1,0:T(8,128)}, f32[640,1152]{1,0:T(8,128)}) custom-call(f32[3]{0:T(128)S(1)} %pad_maximum_fusion.scalars, bf16[640,1152]{1,0:T(8,128)(2,1)S(1)} %get-tuple-element.44.own1.own, bf16[640,1152]{1,0:T(8,128)(2,1)S(1)} %get-tuple-element.28.unit, f32[640,1152]{1,0:T(8,128)S(1)} %shard_map.64.old, ...), custom_call_target="tpu_custom_call" | custom-call | flops 377487360 | bytes 1048576 | tf_op jit(solution)/shard_map/pallas_call | solution.py:151
  86.9 0.0 collective-permute-done.11.refs_1_
  86.9 2.9 %shard_map.63.old = f32[640,1152]{1,0:T(8,128)S(1)} custom-call(f32[3]{0:T(128)S(1)} %pad_maximum_fusion.scalars, bf16[640,1152]{1,0:T(8,128)(2,1)S(1)} %get-tuple-element.23.unit, f32[640,1152]{1,0:T(8,128)S(1)} %shard_map.62.old, bf16[128,1152]{1,0:T(8,128)(2,1)S(1)} %collective-permute-done.10.refs_0_, ...), custom_call_target="tpu_custom_call", output_to_operand_aliasing={{}: (2, {})} | custom-call | flops 1132462080 | bytes 1048576 | tf_op jit(solution)/shard_map/pallas_call | solution.py:151
  89.8 2.9 %collective-permute-done.14.refs_0_ = bf16[128,1152]{1,0:T(8,128)(2,1)S(1)} collective-permute-done((bf16[128,1152]{1,0:T(8,128)(2,1)S(1)}, bf16[128,1152]{1,0:T(8,128)(2,1)S(1)}, u32[]{:S(2)}, u32[]{:S(2)}) %collective-permute-start.14) | collective-permute-done | bytes 294944 | tf_op jit(solution)/shard_map/ppermute | solution.py:258
  92.7 4.2 %shard_map.66 = (f32[640,1152]{1,0:T(8,128)}, f32[640,1152]{1,0:T(8,128)}) custom-call(f32[3]{0:T(128)S(1)} %pad_maximum_fusion.scalars, bf16[640,1152]{1,0:T(8,128)(2,1)S(1)} %get-tuple-element.45.own2.own, bf16[640,1152]{1,0:T(8,128)(2,1)S(1)} %get-tuple-element.23.unit, ...), custom_call_target="tpu_custom_call", output_to_operand_aliasing={{0}: (5, {}), {1}: (6, {})} | custom-call | flops 377487360 | bytes 1048576 | tf_op jit(solution)/shard_map/pallas_call | solution.py:151
  (5 shorter events, 0.0 us)
Async XLA Ops:
  0.6 12.9 %copy-start = (bf16[640,1152]{1,0:T(8,128)(2,1)S(1)}, bf16[640,1152]{1,0:T(8,128)(2,1)}, u32[]{:S(2)}) copy-start(bf16[640,1152]{1,0:T(8,128)(2,1)} %param.5) | copy-start | bytes 4423684
  3.1 26.5 %collective-permute-start.2 = (bf16[256,1152]{1,0:T(8,128)(2,1)}, bf16[256,1152]{1,0:T(8,128)(2,1)}, u32[]{:S(2)}, u32[]{:S(2)}) collective-permute-start(bf16[256,1152]{1,0:T(8,128)(2,1)} %get-tuple-element.47), channel_id=1, source_target_pairs={{0,1},{1,0},{2,3},{3,2},{4,5},{5,4},{6,7},{7,6},{8,9},{9,8},{10,11... | collective-permute-start | bytes 1769480 | tf_op jit(solution)/shard_map/ppermute | solution.py:258
  5.3 10.1 %copy-start.1 = (bf16[640,1152]{1,0:T(8,128)(2,1)S(1)}, bf16[640,1152]{1,0:T(8,128)(2,1)}, u32[]{:S(2)}) copy-start(bf16[640,1152]{1,0:T(8,128)(2,1)} %param.4) | copy-start | bytes 4423684
  5.3 24.4 %collective-permute-start.1 = (bf16[256,1152]{1,0:T(8,128)(2,1)}, bf16[256,1152]{1,0:T(8,128)(2,1)}, u32[]{:S(2)}, u32[]{:S(2)}) collective-permute-start(bf16[256,1152]{1,0:T(8,128)(2,1)} %get-tuple-element.46), channel_id=1, source_target_pairs={{0,62},{1,3},{2,0},{3,5},{4,2},{5,7},{6,4},{7,9},{8,6},{9,11},{10,... | collective-permute-start | bytes 1769480 | tf_op jit(solution)/shard_map/ppermute | solution.py:258
  15.2 37.9 %collective-permute-start = (bf16[640,1152]{1,0:T(8,128)(2,1)S(1)}, bf16[640,1152]{1,0:T(8,128)(2,1)}, u32[]{:S(2)}, u32[]{:S(2)}) collective-permute-start(bf16[640,1152]{1,0:T(8,128)(2,1)S(1)} %get-tuple-element.44.own1.own), channel_id=1, source_target_pairs={{0,2},{1,63},{2,4},{3,1},{4,6},{5,3},{6,8},{7,5},{8,10},{9,7},{10,... | collective-permute-start | bytes 4423688 | tf_op jit(solution)/shard_map/ppermute | solution.py:258
  16.5 17.0 %collective-permute-start.5 = (bf16[256,1152]{1,0:T(8,128)(2,1)}, bf16[256,1152]{1,0:T(8,128)(2,1)S(1)}, u32[]{:S(2)}, u32[]{:S(2)}) collective-permute-start(bf16[256,1152]{1,0:T(8,128)(2,1)} %get-tuple-element.42), channel_id=1, source_target_pairs={{0,1},{1,0},{2,3},{3,2},{4,5},{5,4},{6,7},{7,6},{8,9},{9,8},{10,11... | collective-permute-start | bytes 1769480 | tf_op jit(solution)/shard_map/ppermute | solution.py:258
  18.0 22.3 %collective-permute-start.4 = (bf16[256,1152]{1,0:T(8,128)(2,1)}, bf16[256,1152]{1,0:T(8,128)(2,1)}, u32[]{:S(2)}, u32[]{:S(2)}) collective-permute-start(bf16[256,1152]{1,0:T(8,128)(2,1)} %get-tuple-element.43), channel_id=1, source_target_pairs={{0,62},{1,3},{2,0},{3,5},{4,2},{5,7},{6,4},{7,9},{8,6},{9,11},{10,... | collective-permute-start | bytes 1769480 | tf_op jit(solution)/shard_map/ppermute | solution.py:258
  24.1 5.6 %copy-start.3 = (bf16[128,1152]{1,0:T(8,128)(2,1)S(1)}, bf16[128,1152]{1,0:T(8,128)(2,1)}, u32[]{:S(2)}) copy-start(bf16[128,1152]{1,0:T(8,128)(2,1)} %get-tuple-element.29) | copy-start | bytes 884740
  29.7 16.7 %collective-permute-start.7 = (bf16[128,1152]{1,0:T(8,128)(2,1)S(1)}, bf16[128,1152]{1,0:T(8,128)(2,1)S(1)}, u32[]{:S(2)}, u32[]{:S(2)}) collective-permute-start(bf16[128,1152]{1,0:T(8,128)(2,1)S(1)} %copy-done.3), channel_id=1, source_target_pairs={{0,62},{1,3},{2,0},{3,5},{4,2},{5,7},{6,4},{7,9},{8,6},{9,11},{10,... | collective-permute-start | bytes 884744 | tf_op jit(solution)/shard_map/ppermute | solution.py:258
  33.5 19.6 %collective-permute-start.3 = (bf16[256,1152]{1,0:T(8,128)(2,1)}, bf16[256,1152]{1,0:T(8,128)(2,1)S(1)}, u32[]{:S(2)}, u32[]{:S(2)}) collective-permute-start(bf16[256,1152]{1,0:T(8,128)(2,1)} %collective-permute-done.1.refs_0_), channel_id=1, source_target_pairs={{0,1},{1,0},{2,3},{3,2},{4,5},{5,4},{6,7},{7,6},{8,9},{9,8},{10,11... | collective-permute-start | bytes 1769480 | tf_op jit(solution)/shard_map/ppermute | solution.py:258
  40.3 24.2 %collective-permute-start.9 = (bf16[256,1152]{1,0:T(8,128)(2,1)}, bf16[256,1152]{1,0:T(8,128)(2,1)S(1)}, u32[]{:S(2)}, u32[]{:S(2)}) collective-permute-start(bf16[256,1152]{1,0:T(8,128)(2,1)} %collective-permute-done.2.refs_3_), channel_id=1, source_target_pairs={{0,62},{1,3},{2,0},{3,5},{4,2},{5,7},{6,4},{7,9},{8,6},{9,11},{10,... | collective-permute-start | bytes 1769480 | tf_op jit(solution)/shard_map/ppermute | solution.py:258
  46.1 18.5 %collective-permute-start.6 = (bf16[256,1152]{1,0:T(8,128)(2,1)}, bf16[256,1152]{1,0:T(8,128)(2,1)S(1)}, u32[]{:S(2)}, u32[]{:S(2)}) collective-permute-start(bf16[256,1152]{1,0:T(8,128)(2,1)} %collective-permute-done.4.refs_1_), channel_id=1, source_target_pairs={{0,1},{1,0},{2,3},{3,2},{4,5},{5,4},{6,7},{7,6},{8,9},{9,8},{10,11... | collective-permute-start | bytes 1769480 | tf_op jit(solution)/shard_map/ppermute | solution.py:258
  46.4 12.6 %copy-start.2 = (bf16[128,1152]{1,0:T(8,128)(2,1)S(1)}, bf16[128,1152]{1,0:T(8,128)(2,1)}, u32[]{:S(2)}) copy-start(bf16[128,1152]{1,0:T(8,128)(2,1)} %get-tuple-element.35) | copy-start | bytes 884740
  53.0 18.7 %collective-permute-start.8 = (bf16[256,1152]{1,0:T(8,128)(2,1)S(1)}, bf16[256,1152]{1,0:T(8,128)(2,1)S(1)}, u32[]{:S(2)}, u32[]{:S(2)}) collective-permute-start(bf16[256,1152]{1,0:T(8,128)(2,1)S(1)} %collective-permute-done.3.refs_1_), channel_id=1, source_target_pairs={{0,2},{1,63},{2,4},{3,1},{4,6},{5,3},{6,8},{7,5},{8,10},{9,7},{10,... | collective-permute-start | bytes 1769480 | tf_op jit(solution)/shard_map/ppermute | solution.py:258
  53.1 25.1 %collective-permute-start.12 = (bf16[256,1152]{1,0:T(8,128)(2,1)S(1)}, bf16[256,1152]{1,0:T(8,128)(2,1)S(1)}, u32[]{:S(2)}, u32[]{:S(2)}) collective-permute-start(bf16[256,1152]{1,0:T(8,128)(2,1)S(1)} %collective-permute-done.5.refs_4_), channel_id=1, source_target_pairs={{0,62},{1,3},{2,0},{3,5},{4,2},{5,7},{6,4},{7,9},{8,6},{9,11},{10,... | collective-permute-start | bytes 1769480 | tf_op jit(solution)/shard_map/ppermute | solution.py:258
  59.0 15.8 %collective-permute-start.13 = (bf16[128,1152]{1,0:T(8,128)(2,1)S(1)}, bf16[128,1152]{1,0:T(8,128)(2,1)S(1)}, u32[]{:S(2)}, u32[]{:S(2)}) collective-permute-start(bf16[128,1152]{1,0:T(8,128)(2,1)S(1)} %copy-done.2), channel_id=1, source_target_pairs={{0,1},{1,0},{2,3},{3,2},{4,5},{5,4},{6,7},{7,6},{8,9},{9,8},{10,11... | collective-permute-start | bytes 884744 | tf_op jit(solution)/shard_map/ppermute | solution.py:258
  64.5 22.3 %collective-permute-start.11 = (bf16[256,1152]{1,0:T(8,128)(2,1)S(1)}, bf16[256,1152]{1,0:T(8,128)(2,1)S(1)}, u32[]{:S(2)}, u32[]{:S(2)}) collective-permute-start(bf16[256,1152]{1,0:T(8,128)(2,1)S(1)} %collective-permute-done.6.refs_0_), channel_id=1, source_target_pairs={{0,2},{1,63},{2,4},{3,1},{4,6},{5,3},{6,8},{7,5},{8,10},{9,7},{10,... | collective-permute-start | bytes 1769480 | tf_op jit(solution)/shard_map/ppermute | solution.py:258
  64.6 17.7 %collective-permute-start.10 = (bf16[128,1152]{1,0:T(8,128)(2,1)S(1)}, bf16[128,1152]{1,0:T(8,128)(2,1)S(1)}, u32[]{:S(2)}, u32[]{:S(2)}) collective-permute-start(bf16[128,1152]{1,0:T(8,128)(2,1)S(1)} %collective-permute-done.7.refs_2_), channel_id=1, source_target_pairs={{0,1},{1,0},{2,3},{3,2},{4,5},{5,4},{6,7},{7,6},{8,9},{9,8},{10,11... | collective-permute-start | bytes 884744 | tf_op jit(solution)/shard_map/ppermute | solution.py:258
  74.9 7.8 %collective-permute-start.15 = (bf16[128,1152]{1,0:T(8,128)(2,1)S(1)}, bf16[128,1152]{1,0:T(8,128)(2,1)S(1)}, u32[]{:S(2)}, u32[]{:S(2)}) collective-permute-start(bf16[128,1152]{1,0:T(8,128)(2,1)S(1)} %collective-permute-done.13.refs_2_), channel_id=1, source_target_pairs={{0,62},{1,3},{2,0},{3,5},{4,2},{5,7},{6,4},{7,9},{8,6},{9,11},{10,... | collective-permute-start | bytes 884744 | tf_op jit(solution)/shard_map/ppermute | solution.py:258
  82.3 10.4 %collective-permute-start.14 = (bf16[128,1152]{1,0:T(8,128)(2,1)S(1)}, bf16[128,1152]{1,0:T(8,128)(2,1)S(1)}, u32[]{:S(2)}, u32[]{:S(2)}) collective-permute-start(bf16[128,1152]{1,0:T(8,128)(2,1)S(1)} %collective-permute-done.10.refs_0_), channel_id=1, source_target_pairs={{0,2},{1,63},{2,4},{3,1},{4,6},{5,3},{6,8},{7,5},{8,10},{9,7},{10,... | collective-permute-start | bytes 884744 | tf_op jit(solution)/shard_map/ppermute | solution.py:258
where the time goes:
time: 97.3 us; the launch traced here: 97.1 us
  starting transfers between devices  40.7 us (42%)
  Pallas kernels  36.1 us (37%)
  waiting for transfers between devices  11.7 us (12%)
  other arithmetic  6.25 us (6%)
  between operations  2.35 us (2%)
    ppermute x16, starting transfers between devices, shards(): there[n] = lax.ppermute(value, 'blk', routes[n[0]])  40.7 us
    pallas_call x8, Pallas kernels, call(): pl.pallas_call(kernel, in_specs=specs, out_specs=out_specs, out_shape=out...  36.1 us
    ppermute x16, waiting for transfers between devices, shards(): there[n] = lax.ppermute(value, 'blk', routes[n[0]])  11.7 us
    select_n x3, other arithmetic, one(): return jnp.where(even, caption[a:b], visual[a:b])  3.7 us
    select_n x1, other arithmetic, two(): return jnp.where(even, visual[a:b], caption[a:b])  2.47 us
  transfers between devices with their start and end apart: 16, of which 4 were waited for; matrix products, arithmetic and copies ran while one was open for 4% of the time, Pallas kernels for 33%

commit v1 on v0

--- a/solution.py
+++ b/solution.py
@@ -49,7 +49,7 @@
     products = lax.dot_general(
         own, partners, (((1,), (1,)), ((), ())), preferred_element_type=jnp.float32
     )
-    exponents = products * (-LOG2_E * scalars[0]) - LOG2_E * scalars[1]
+    exponents = products * (-LOG2_E * scalars[0:1, 0:1]) - LOG2_E * scalars[1:2, 0:1]
     if first_row is not None:
         rows = lax.broadcasted_iota(jnp.int32, products.shape, 0) + first_row
         same = rows == lax.broadcasted_iota(jnp.int32, products.shape, 1)
@@ -108,7 +108,7 @@
     for a in range(0, rows, step):
         piece = pl.ds(a, step)
         units, inverse = normalized(own[piece, :])
-        gradient = scalars[0] * sums[piece, :]
+        gradient = scalars[0:1, 0:1] * sums[piece, :]
         along = jnp.sum(units * gradient, axis=1, keepdims=True)
         sums[piece, :] = (gradient - units * along) * inverse
 
@@ -137,12 +137,11 @@
     fill(scratch, refs[:n])
     for rows in tiles(unit.shape[0]):
         total[rows, :] = old[rows, :] + against(scalars, unit[rows, :], scratch[...])
-    first = scalars[2] > 0.5 if side == 1 else scalars[2] < 0.5
+    first = jnp.max(scalars[2:3, :]) > 0.5 if side == 1 else jnp.max(scalars[2:3, :]) < 0.5
     project(scalars, own, total, first, (out0, out1), semaphores)
 
 
 VMEM = pl.BlockSpec(memory_space=pltpu.VMEM)
-SMEM = pl.BlockSpec(memory_space=pltpu.SMEM)
 HBM = pl.BlockSpec(memory_space=pl.ANY)
 
 
@@ -189,7 +188,8 @@
     caption, visual = lax.optimization_barrier((caption, visual, heads))[:2]
     own1, own2 = one(0, rows), two(0, rows)
     flag = jnp.where(even, 0.0, 1.0)
-    scalars = jnp.stack([sharpness_scale[0], score_shift[0], flag])
+    row = lax.broadcasted_iota(jnp.int32, (8, 128), 0)
+    scalars = jnp.where(row == 0, sharpness_scale[0], jnp.where(row == 1, score_shift[0], flag))
 
     real = jax.ShapeDtypeStruct((rows, width), jnp.float32)
     half = jax.ShapeDtypeStruct((rows, width), jnp.bfloat16)
@@ -205,7 +205,7 @@
         return call(
             functools.partial(middle_kernel, len(partners)),
             operands,
-            [SMEM] + [VMEM] * (len(operands) - 1),
+            [VMEM] + [VMEM] * (len(operands) - 1),
             real,
             VMEM,
             [units_of(partners)],
@@ -219,7 +219,7 @@
         return call(
             functools.partial(last_kernel, len(partners), side),
             operands,
-            [SMEM] + [VMEM] * (n - 1 - len(outs)) + [HBM] * len(outs),
+            [VMEM] + [VMEM] * (n - 1 - len(outs)) + [HBM] * len(outs),
             (real, real),
             (HBM, HBM),
             [units_of(partners), *staging],
@@ -260,7 +260,7 @@
             units[1], units[2], sums[1], sums[2] = call(
                 first_kernel,
                 [scalars, own1, own2],
-                [SMEM, VMEM, VMEM],
+                [VMEM, VMEM, VMEM],
                 (half, half, real, real),
                 (VMEM,) * 4,
                 [pltpu.VMEM((rows, rows), jnp.bfloat16)],

time: 97.3 us -> 95.7 us (0.984)
  Pallas kernels: 36.1 us -> 33 us
  waiting for transfers between devices: 11.7 us -> 12.8 us
    pallas_call x8, Pallas kernels: 36.1 us -> 33 us  [call(): pl.pallas_call(kernel, in_specs=specs, out_specs=out_specs, out_shape=out...]
    ppermute x16, waiting for transfers between devices: 11.7 us -> 12.8 us  [shards(): there[n] = lax.ppermute(value, 'blk', routes[n[0]])]
  transfers between devices with their start and end apart: 16 -> 16, of which waited for: 4 -> 5; matrix products, arithmetic and copies ran while one was open for 4% -> 4% of each run, Pallas kernels for 33% -> 31%
where the time goes in v1:
time: 95.7 us; the launch traced here: 95.5 us
  starting transfers between devices  41.2 us (43%)
  Pallas kernels  33 us (34%)
  waiting for transfers between devices  12.8 us (13%)
  other arithmetic  6.25 us (7%)
  between operations  2.35 us (2%)
    ppermute x16, starting transfers between devices, shards(): there[n] = lax.ppermute(value, 'blk', routes[n[0]])  41.2 us
    pallas_call x8, Pallas kernels, call(): pl.pallas_call(kernel, in_specs=specs, out_specs=out_specs, out_shape=out...  33 us
    ppermute x16, waiting for transfers between devices, shards(): there[n] = lax.ppermute(value, 'blk', routes[n[0]])  12.8 us
    select_n x3, other arithmetic, one(): return jnp.where(even, caption[a:b], visual[a:b])  3.7 us
    select_n x1, other arithmetic, two(): return jnp.where(even, visual[a:b], caption[a:b])  2.47 us
  transfers between devices with their start and end apart: 16, of which 5 were waited for; matrix products, arithmetic and copies ran while one was open for 4% of the time, Pallas kernels for 31%

profile of v1, /device:TPU:2, one launch (start us, length us, event | category | flops | bytes accessed | tf_op | source)
XLA Modules:
  0.0 95.5 jit_solution(7760710713485089649)
XLA Ops:
  0.6 0.0 copy-start
  0.7 2.5 %broadcast_select_fusion.4 = (bf16[256,1152]{1,0:T(8,128)(2,1)}, bf16[256,1152]{1,0:T(8,128)(2,1)}) fusion(pred[]{:T(512)S(6)} %eq.23, bf16[640,1152]{1,0:T(8,128)(2,1)} %param.4, bf16[640,1152]{1,0:T(8,128)(2,1)} %param.5), kind=kLoop, calls=%fused_computation.4 | loop fusion | flops 589824 | bytes 2359297 | tf_op jit(solution)/shard_map/jit(_where)/select_n | solution.py:181
  3.1 2.1 %collective-permute-start.2 = (bf16[256,1152]{1,0:T(8,128)(2,1)}, bf16[256,1152]{1,0:T(8,128)(2,1)}, u32[]{:S(2)}, u32[]{:S(2)}) collective-permute-start(bf16[256,1152]{1,0:T(8,128)(2,1)} %get-tuple-element.47), channel_id=1, source_target_pairs={{0,1},{1,0},{2,3},{3,2},{4,5},{5,4},{6,7},{7,6},{8,9},{9,8},{10,11... | collective-permute-start | bytes 1769480 | tf_op jit(solution)/shard_map/ppermute | solution.py:258
  5.3 8.3 %collective-permute-start.1 = (bf16[256,1152]{1,0:T(8,128)(2,1)}, bf16[256,1152]{1,0:T(8,128)(2,1)}, u32[]{:S(2)}, u32[]{:S(2)}) collective-permute-start(bf16[256,1152]{1,0:T(8,128)(2,1)} %get-tuple-element.46), channel_id=1, source_target_pairs={{0,62},{1,3},{2,0},{3,5},{4,2},{5,7},{6,4},{7,9},{8,6},{9,11},{10,... | collective-permute-start | bytes 1769480 | tf_op jit(solution)/shard_map/ppermute | solution.py:258
  13.6 0.0 copy-done
  13.6 1.7 %broadcast_select_fusion = (bf16[640,1152]{1,0:T(8,128)(2,1)S(1)}, bf16[640,1152]{1,0:T(8,128)(2,1)S(1)}) fusion(bf16[640,1152]{1,0:T(8,128)(2,1)S(1)} %copy-done, bf16[640,1152]{1,0:T(8,128)(2,1)} %param.4, pred[]{:T(512)S(6)} %eq.23), kind=kLoop, calls=%fused_computation | loop fusion | flops 1474560 | bytes 5898241 | tf_op jit(solution)/shard_map/jit(_where)/select_n | solution.py:178
  15.2 0.1 collective-permute-start
  15.3 1.1 %broadcast_select_fusion.2 = (bf16[256,1152]{1,0:T(8,128)(2,1)}, bf16[256,1152]{1,0:T(8,128)(2,1)}) fusion(pred[]{:T(512)S(6)} %eq.23, bf16[640,1152]{1,0:T(8,128)(2,1)S(1)} %copy-done, bf16[640,1152]{1,0:T(8,128)(2,1)S(1)} %copy-done.1), kind=kLoop, calls=%fused_computation.2 | loop fusion | flops 589824 | bytes 2359297 | tf_op jit(solution)/shard_map/jit(_where)/select_n | solution.py:178
  16.5 1.5 %collective-permute-start.5 = (bf16[256,1152]{1,0:T(8,128)(2,1)}, bf16[256,1152]{1,0:T(8,128)(2,1)S(1)}, u32[]{:S(2)}, u32[]{:S(2)}) collective-permute-start(bf16[256,1152]{1,0:T(8,128)(2,1)} %get-tuple-element.42), channel_id=1, source_target_pairs={{0,1},{1,0},{2,3},{3,2},{4,5},{5,4},{6,7},{7,6},{8,9},{9,8},{10,11... | collective-permute-start | bytes 1769480 | tf_op jit(solution)/shard_map/ppermute | solution.py:258
  18.0 3.8 %collective-permute-start.4 = (bf16[256,1152]{1,0:T(8,128)(2,1)}, bf16[256,1152]{1,0:T(8,128)(2,1)}, u32[]{:S(2)}, u32[]{:S(2)}) collective-permute-start(bf16[256,1152]{1,0:T(8,128)(2,1)} %get-tuple-element.43), channel_id=1, source_target_pairs={{0,62},{1,3},{2,0},{3,5},{4,2},{5,7},{6,4},{7,9},{8,6},{9,11},{10,... | collective-permute-start | bytes 1769480 | tf_op jit(solution)/shard_map/ppermute | solution.py:258
  21.8 0.9 broadcast_select_fusion.6
  24.0 0.1 broadcast_select_fusion.8.scalars
  24.1 5.0 %shard_map.59 = (bf16[640,1152]{1,0:T(8,128)(2,1)S(1)}, bf16[640,1152]{1,0:T(8,128)(2,1)S(1)}, f32[640,1152]{1,0:T(8,128)S(1)}, f32[640,1152]{1,0:T(8,128)S(1)}) custom-call(f32[8,128]{1,0:T(8,128)S(1)} %broadcast_select_fusion.8.scalars, bf16[640,1152]{1,0:T(8,128)(2,1)S(1)} %get-tuple-element.44.own1.own, bf16[640,1152]{1,0:T(8,128)(2,1)S(1)} %get-tuple-element.45.own2.own), custom_call_target="tpu_custom_call" | custom-call | flops 3774873600 | bytes 1048576 | tf_op jit(solution)/shard_map/pallas_call | solution.py:150
  29.1 0.0 collective-permute-done.2.refs_3_
  29.1 0.0 collective-permute-done.1.refs_0_
  29.1 0.0 copy-done.3
  29.2 4.3 %collective-permute-start.7 = (bf16[128,1152]{1,0:T(8,128)(2,1)S(1)}, bf16[128,1152]{1,0:T(8,128)(2,1)S(1)}, u32[]{:S(2)}, u32[]{:S(2)}) collective-permute-start(bf16[128,1152]{1,0:T(8,128)(2,1)S(1)} %copy-done.3), channel_id=1, source_target_pairs={{0,62},{1,3},{2,0},{3,5},{4,2},{5,7},{6,4},{7,9},{8,6},{9,11},{10,... | collective-permute-start | bytes 884744 | tf_op jit(solution)/shard_map/ppermute | solution.py:258
  33.5 0.0 collective-permute-start.3
  33.5 0.0 collective-permute-done.5.refs_4_
  33.5 6.8 %collective-permute-done.4.refs_1_ = bf16[256,1152]{1,0:T(8,128)(2,1)} collective-permute-done((bf16[256,1152]{1,0:T(8,128)(2,1)}, bf16[256,1152]{1,0:T(8,128)(2,1)}, u32[]{:S(2)}, u32[]{:S(2)}) %collective-permute-start.4) | collective-permute-done | bytes 589856 | tf_op jit(solution)/shard_map/ppermute | solution.py:258
  40.3 5.8 %collective-permute-start.9 = (bf16[256,1152]{1,0:T(8,128)(2,1)}, bf16[256,1152]{1,0:T(8,128)(2,1)S(1)}, u32[]{:S(2)}, u32[]{:S(2)}) collective-permute-start(bf16[256,1152]{1,0:T(8,128)(2,1)} %collective-permute-done.2.refs_3_), channel_id=1, source_target_pairs={{0,62},{1,3},{2,0},{3,5},{4,2},{5,7},{6,4},{7,9},{8,6},{9,11},{10,... | collective-permute-start | bytes 1769480 | tf_op jit(solution)/shard_map/ppermute | solution.py:258
  46.1 0.0 collective-permute-start.6
  46.1 0.3 collective-permute-done.7.refs_2_
  46.4 6.6 %shard_map.61.old = f32[640,1152]{1,0:T(8,128)S(1)} custom-call(f32[8,128]{1,0:T(8,128)S(1)} %broadcast_select_fusion.8.scalars, bf16[640,1152]{1,0:T(8,128)(2,1)S(1)} %get-tuple-element.28.unit, f32[640,1152]{1,0:T(8,128)S(1)} %get-tuple-element.25.old, bf16[256,1152]{1,0:T(8,128)(2,1)} %collective-permute-done.1.refs_0_, ...), custom_call_target="tpu_custom_call", output_to_operand_aliasing={{}: (2, {})} | custom-call | flops 3397386240 | bytes 1048576 | tf_op jit(solution)/shard_map/pallas_call | solution.py:150
  53.0 0.0 collective-permute-done.3.refs_1_
  53.0 0.1 collective-permute-start.8
  53.1 0.0 collective-permute-done.refs_0_
  53.1 5.9 %collective-permute-start.12 = (bf16[256,1152]{1,0:T(8,128)(2,1)S(1)}, bf16[256,1152]{1,0:T(8,128)(2,1)S(1)}, u32[]{:S(2)}, u32[]{:S(2)}) collective-permute-start(bf16[256,1152]{1,0:T(8,128)(2,1)S(1)} %collective-permute-done.5.refs_4_), channel_id=1, source_target_pairs={{0,62},{1,3},{2,0},{3,5},{4,2},{5,7},{6,4},{7,9},{8,6},{9,11},{10,... | collective-permute-start | bytes 1769480 | tf_op jit(solution)/shard_map/ppermute | solution.py:258
  59.0 0.0 collective-permute-start.13
  59.0 5.5 %shard_map.60.old = f32[640,1152]{1,0:T(8,128)S(1)} custom-call(f32[8,128]{1,0:T(8,128)S(1)} %broadcast_select_fusion.8.scalars, bf16[640,1152]{1,0:T(8,128)(2,1)S(1)} %get-tuple-element.23.unit, f32[640,1152]{1,0:T(8,128)S(1)} %get-tuple-element.24.old, bf16[640,1152]{1,0:T(8,128)(2,1)} %collective-permute-done.refs_0_, ...), custom_call_target="tpu_custom_call", output_to_operand_aliasing={{}: (2, {})} | custom-call | flops 2642411520 | bytes 1048576 | tf_op jit(solution)/shard_map/pallas_call | solution.py:150
  64.5 0.0 collective-permute-done.9.refs_0_
  64.5 0.0 collective-permute-done.6.refs_0_
  64.6 0.1 collective-permute-start.11
  64.7 5.4 %collective-permute-start.10 = (bf16[128,1152]{1,0:T(8,128)(2,1)S(1)}, bf16[128,1152]{1,0:T(8,128)(2,1)S(1)}, u32[]{:S(2)}, u32[]{:S(2)}) collective-permute-start(bf16[128,1152]{1,0:T(8,128)(2,1)S(1)} %collective-permute-done.7.refs_2_), channel_id=1, source_target_pairs={{0,1},{1,0},{2,3},{3,2},{4,5},{5,4},{6,7},{7,6},{8,9},{9,8},{10,11... | collective-permute-start | bytes 884744 | tf_op jit(solution)/shard_map/ppermute | solution.py:258
  70.1 1.6 %collective-permute-done.8.refs_1_ = bf16[256,1152]{1,0:T(8,128)(2,1)S(1)} collective-permute-done((bf16[256,1152]{1,0:T(8,128)(2,1)S(1)}, bf16[256,1152]{1,0:T(8,128)(2,1)S(1)}, u32[]{:S(2)}, u32[]{:S(2)}) %collective-permute-start.8) | collective-permute-done | bytes 589856 | tf_op jit(solution)/shard_map/ppermute | solution.py:258
  71.7 2.6 %shard_map.62.old = f32[640,1152]{1,0:T(8,128)S(1)} custom-call(f32[8,128]{1,0:T(8,128)S(1)} %broadcast_select_fusion.8.scalars, bf16[640,1152]{1,0:T(8,128)(2,1)S(1)} %get-tuple-element.23.unit, f32[640,1152]{1,0:T(8,128)S(1)} %shard_map.60.old, bf16[256,1152]{1,0:T(8,128)(2,1)S(1)} %collective-permute-done.6.refs_0_, ...), custom_call_target="tpu_custom_call", output_to_operand_aliasing={{}: (2, {})} | custom-call | flops 1509949440 | bytes 1048576 | tf_op jit(solution)/shard_map/pallas_call | solution.py:150
  74.3 0.0 collective-permute-done.13.refs_2_
  74.3 3.4 %collective-permute-start.15 = (bf16[128,1152]{1,0:T(8,128)(2,1)S(1)}, bf16[128,1152]{1,0:T(8,128)(2,1)S(1)}, u32[]{:S(2)}, u32[]{:S(2)}) collective-permute-start(bf16[128,1152]{1,0:T(8,128)(2,1)S(1)} %collective-permute-done.13.refs_2_), channel_id=1, source_target_pairs={{0,62},{1,3},{2,0},{3,5},{4,2},{5,7},{6,4},{7,9},{8,6},{9,11},{10,... | collective-permute-start | bytes 884744 | tf_op jit(solution)/shard_map/ppermute | solution.py:258
  77.7 0.0 collective-permute-done.12.refs_1_
  77.7 3.5 %shard_map.64.old = f32[640,1152]{1,0:T(8,128)S(1)} custom-call(f32[8,128]{1,0:T(8,128)S(1)} %broadcast_select_fusion.8.scalars, bf16[640,1152]{1,0:T(8,128)(2,1)S(1)} %get-tuple-element.28.unit, f32[640,1152]{1,0:T(8,128)S(1)} %shard_map.61.old, bf16[256,1152]{1,0:T(8,128)(2,1)S(1)} %collective-permute-done.9.refs_0_, ...), custom_call_target="tpu_custom_call", output_to_operand_aliasing={{}: (2, {})} | custom-call | flops 1887436800 | bytes 1048576 | tf_op jit(solution)/shard_map/pallas_call | solution.py:150
  81.3 0.0 collective-permute-done.10.refs_0_
  81.3 0.3 collective-permute-start.14
  81.6 0.4 collective-permute-done.15.refs_0_
  82.0 3.7 %shard_map.65 = (f32[640,1152]{1,0:T(8,128)}, f32[640,1152]{1,0:T(8,128)}) custom-call(f32[8,128]{1,0:T(8,128)S(1)} %broadcast_select_fusion.8.scalars, bf16[640,1152]{1,0:T(8,128)(2,1)S(1)} %get-tuple-element.44.own1.own, bf16[640,1152]{1,0:T(8,128)(2,1)S(1)} %get-tuple-element.28.unit, f32[640,1152]{1,0:T(8,128)S(1)} %shard_map.64.old, ...), custom_call_target="tpu_custom_call" | custom-call | flops 377487360 | bytes 1048576 | tf_op jit(solution)/shard_map/pallas_call | solution.py:150
  85.7 0.0 collective-permute-done.11.refs_1_
  85.7 2.4 %shard_map.63.old = f32[640,1152]{1,0:T(8,128)S(1)} custom-call(f32[8,128]{1,0:T(8,128)S(1)} %broadcast_select_fusion.8.scalars, bf16[640,1152]{1,0:T(8,128)(2,1)S(1)} %get-tuple-element.23.unit, f32[640,1152]{1,0:T(8,128)S(1)} %shard_map.62.old, bf16[128,1152]{1,0:T(8,128)(2,1)S(1)} %collective-permute-done.10.refs_0_, ...), custom_call_target="tpu_custom_call", output_to_operand_aliasing={{}: (2, {})} | custom-call | flops 1132462080 | bytes 1048576 | tf_op jit(solution)/shard_map/pallas_call | solution.py:150
  88.1 3.6 %collective-permute-done.14.refs_0_ = bf16[128,1152]{1,0:T(8,128)(2,1)S(1)} collective-permute-done((bf16[128,1152]{1,0:T(8,128)(2,1)S(1)}, bf16[128,1152]{1,0:T(8,128)(2,1)S(1)}, u32[]{:S(2)}, u32[]{:S(2)}) %collective-permute-start.14) | collective-permute-done | bytes 294944 | tf_op jit(solution)/shard_map/ppermute | solution.py:258
  91.6 3.7 %shard_map.66 = (f32[640,1152]{1,0:T(8,128)}, f32[640,1152]{1,0:T(8,128)}) custom-call(f32[8,128]{1,0:T(8,128)S(1)} %broadcast_select_fusion.8.scalars, bf16[640,1152]{1,0:T(8,128)(2,1)S(1)} %get-tuple-element.45.own2.own, bf16[640,1152]{1,0:T(8,128)(2,1)S(1)} %get-tuple-element.23.unit, ...), custom_call_target="tpu_custom_call", output_to_operand_aliasing={{0}: (5, {}), {1}: (6, {})} | custom-call | flops 377487360 | bytes 1048576 | tf_op jit(solution)/shard_map/pallas_call | solution.py:150
  (7 shorter events, 0.0 us)
Async XLA Ops:
  0.6 12.9 %copy-start = (bf16[640,1152]{1,0:T(8,128)(2,1)S(1)}, bf16[640,1152]{1,0:T(8,128)(2,1)}, u32[]{:S(2)}) copy-start(bf16[640,1152]{1,0:T(8,128)(2,1)} %param.5) | copy-start | bytes 4423684
  3.1 26.0 %collective-permute-start.2 = (bf16[256,1152]{1,0:T(8,128)(2,1)}, bf16[256,1152]{1,0:T(8,128)(2,1)}, u32[]{:S(2)}, u32[]{:S(2)}) collective-permute-start(bf16[256,1152]{1,0:T(8,128)(2,1)} %get-tuple-element.47), channel_id=1, source_target_pairs={{0,1},{1,0},{2,3},{3,2},{4,5},{5,4},{6,7},{7,6},{8,9},{9,8},{10,11... | collective-permute-start | bytes 1769480 | tf_op jit(solution)/shard_map/ppermute | solution.py:258
  5.3 10.1 %copy-start.1 = (bf16[640,1152]{1,0:T(8,128)(2,1)S(1)}, bf16[640,1152]{1,0:T(8,128)(2,1)}, u32[]{:S(2)}) copy-start(bf16[640,1152]{1,0:T(8,128)(2,1)} %param.4) | copy-start | bytes 4423684
  5.3 23.9 %collective-permute-start.1 = (bf16[256,1152]{1,0:T(8,128)(2,1)}, bf16[256,1152]{1,0:T(8,128)(2,1)}, u32[]{:S(2)}, u32[]{:S(2)}) collective-permute-start(bf16[256,1152]{1,0:T(8,128)(2,1)} %get-tuple-element.46), channel_id=1, source_target_pairs={{0,62},{1,3},{2,0},{3,5},{4,2},{5,7},{6,4},{7,9},{8,6},{9,11},{10,... | collective-permute-start | bytes 1769480 | tf_op jit(solution)/shard_map/ppermute | solution.py:258
  15.2 37.9 %collective-permute-start = (bf16[640,1152]{1,0:T(8,128)(2,1)S(1)}, bf16[640,1152]{1,0:T(8,128)(2,1)}, u32[]{:S(2)}, u32[]{:S(2)}) collective-permute-start(bf16[640,1152]{1,0:T(8,128)(2,1)S(1)} %get-tuple-element.44.own1.own), channel_id=1, source_target_pairs={{0,2},{1,63},{2,4},{3,1},{4,6},{5,3},{6,8},{7,5},{8,10},{9,7},{10,... | collective-permute-start | bytes 4423688 | tf_op jit(solution)/shard_map/ppermute | solution.py:258
  16.5 17.0 %collective-permute-start.5 = (bf16[256,1152]{1,0:T(8,128)(2,1)}, bf16[256,1152]{1,0:T(8,128)(2,1)S(1)}, u32[]{:S(2)}, u32[]{:S(2)}) collective-permute-start(bf16[256,1152]{1,0:T(8,128)(2,1)} %get-tuple-element.42), channel_id=1, source_target_pairs={{0,1},{1,0},{2,3},{3,2},{4,5},{5,4},{6,7},{7,6},{8,9},{9,8},{10,11... | collective-permute-start | bytes 1769480 | tf_op jit(solution)/shard_map/ppermute | solution.py:258
  18.0 22.3 %collective-permute-start.4 = (bf16[256,1152]{1,0:T(8,128)(2,1)}, bf16[256,1152]{1,0:T(8,128)(2,1)}, u32[]{:S(2)}, u32[]{:S(2)}) collective-permute-start(bf16[256,1152]{1,0:T(8,128)(2,1)} %get-tuple-element.43), channel_id=1, source_target_pairs={{0,62},{1,3},{2,0},{3,5},{4,2},{5,7},{6,4},{7,9},{8,6},{9,11},{10,... | collective-permute-start | bytes 1769480 | tf_op jit(solution)/shard_map/ppermute | solution.py:258
  24.1 5.1 %copy-start.3 = (bf16[128,1152]{1,0:T(8,128)(2,1)S(1)}, bf16[128,1152]{1,0:T(8,128)(2,1)}, u32[]{:S(2)}) copy-start(bf16[128,1152]{1,0:T(8,128)(2,1)} %get-tuple-element.29) | copy-start | bytes 884740
  29.2 17.3 %collective-permute-start.7 = (bf16[128,1152]{1,0:T(8,128)(2,1)S(1)}, bf16[128,1152]{1,0:T(8,128)(2,1)S(1)}, u32[]{:S(2)}, u32[]{:S(2)}) collective-permute-start(bf16[128,1152]{1,0:T(8,128)(2,1)S(1)} %copy-done.3), channel_id=1, source_target_pairs={{0,62},{1,3},{2,0},{3,5},{4,2},{5,7},{6,4},{7,9},{8,6},{9,11},{10,... | collective-permute-start | bytes 884744 | tf_op jit(solution)/shard_map/ppermute | solution.py:258
  33.5 19.6 %collective-permute-start.3 = (bf16[256,1152]{1,0:T(8,128)(2,1)}, bf16[256,1152]{1,0:T(8,128)(2,1)S(1)}, u32[]{:S(2)}, u32[]{:S(2)}) collective-permute-start(bf16[256,1152]{1,0:T(8,128)(2,1)} %collective-permute-done.1.refs_0_), channel_id=1, source_target_pairs={{0,1},{1,0},{2,3},{3,2},{4,5},{5,4},{6,7},{7,6},{8,9},{9,8},{10,11... | collective-permute-start | bytes 1769480 | tf_op jit(solution)/shard_map/ppermute | solution.py:258
  40.3 24.3 %collective-permute-start.9 = (bf16[256,1152]{1,0:T(8,128)(2,1)}, bf16[256,1152]{1,0:T(8,128)(2,1)S(1)}, u32[]{:S(2)}, u32[]{:S(2)}) collective-permute-start(bf16[256,1152]{1,0:T(8,128)(2,1)} %collective-permute-done.2.refs_3_), channel_id=1, source_target_pairs={{0,62},{1,3},{2,0},{3,5},{4,2},{5,7},{6,4},{7,9},{8,6},{9,11},{10,... | collective-permute-start | bytes 1769480 | tf_op jit(solution)/shard_map/ppermute | solution.py:258
  46.1 18.5 %collective-permute-start.6 = (bf16[256,1152]{1,0:T(8,128)(2,1)}, bf16[256,1152]{1,0:T(8,128)(2,1)S(1)}, u32[]{:S(2)}, u32[]{:S(2)}) collective-permute-start(bf16[256,1152]{1,0:T(8,128)(2,1)} %collective-permute-done.4.refs_1_), channel_id=1, source_target_pairs={{0,1},{1,0},{2,3},{3,2},{4,5},{5,4},{6,7},{7,6},{8,9},{9,8},{10,11... | collective-permute-start | bytes 1769480 | tf_op jit(solution)/shard_map/ppermute | solution.py:258
  46.4 12.6 %copy-start.2 = (bf16[128,1152]{1,0:T(8,128)(2,1)S(1)}, bf16[128,1152]{1,0:T(8,128)(2,1)}, u32[]{:S(2)}) copy-start(bf16[128,1152]{1,0:T(8,128)(2,1)} %get-tuple-element.35) | copy-start | bytes 884740
  53.0 18.7 %collective-permute-start.8 = (bf16[256,1152]{1,0:T(8,128)(2,1)S(1)}, bf16[256,1152]{1,0:T(8,128)(2,1)S(1)}, u32[]{:S(2)}, u32[]{:S(2)}) collective-permute-start(bf16[256,1152]{1,0:T(8,128)(2,1)S(1)} %collective-permute-done.3.refs_1_), channel_id=1, source_target_pairs={{0,2},{1,63},{2,4},{3,1},{4,6},{5,3},{6,8},{7,5},{8,10},{9,7},{10,... | collective-permute-start | bytes 1769480 | tf_op jit(solution)/shard_map/ppermute | solution.py:258
  53.1 24.6 %collective-permute-start.12 = (bf16[256,1152]{1,0:T(8,128)(2,1)S(1)}, bf16[256,1152]{1,0:T(8,128)(2,1)S(1)}, u32[]{:S(2)}, u32[]{:S(2)}) collective-permute-start(bf16[256,1152]{1,0:T(8,128)(2,1)S(1)} %collective-permute-done.5.refs_4_), channel_id=1, source_target_pairs={{0,62},{1,3},{2,0},{3,5},{4,2},{5,7},{6,4},{7,9},{8,6},{9,11},{10,... | collective-permute-start | bytes 1769480 | tf_op jit(solution)/shard_map/ppermute | solution.py:258
  59.0 15.3 %collective-permute-start.13 = (bf16[128,1152]{1,0:T(8,128)(2,1)S(1)}, bf16[128,1152]{1,0:T(8,128)(2,1)S(1)}, u32[]{:S(2)}, u32[]{:S(2)}) collective-permute-start(bf16[128,1152]{1,0:T(8,128)(2,1)S(1)} %copy-done.2), channel_id=1, source_target_pairs={{0,1},{1,0},{2,3},{3,2},{4,5},{5,4},{6,7},{7,6},{8,9},{9,8},{10,11... | collective-permute-start | bytes 884744 | tf_op jit(solution)/shard_map/ppermute | solution.py:258
  64.6 21.1 %collective-permute-start.11 = (bf16[256,1152]{1,0:T(8,128)(2,1)S(1)}, bf16[256,1152]{1,0:T(8,128)(2,1)S(1)}, u32[]{:S(2)}, u32[]{:S(2)}) collective-permute-start(bf16[256,1152]{1,0:T(8,128)(2,1)S(1)} %collective-permute-done.6.refs_0_), channel_id=1, source_target_pairs={{0,2},{1,63},{2,4},{3,1},{4,6},{5,3},{6,8},{7,5},{8,10},{9,7},{10,... | collective-permute-start | bytes 1769480 | tf_op jit(solution)/shard_map/ppermute | solution.py:258
  64.7 16.6 %collective-permute-start.10 = (bf16[128,1152]{1,0:T(8,128)(2,1)S(1)}, bf16[128,1152]{1,0:T(8,128)(2,1)S(1)}, u32[]{:S(2)}, u32[]{:S(2)}) collective-permute-start(bf16[128,1152]{1,0:T(8,128)(2,1)S(1)} %collective-permute-done.7.refs_2_), channel_id=1, source_target_pairs={{0,1},{1,0},{2,3},{3,2},{4,5},{5,4},{6,7},{7,6},{8,9},{9,8},{10,11... | collective-permute-start | bytes 884744 | tf_op jit(solution)/shard_map/ppermute | solution.py:258
  74.3 7.6 %collective-permute-start.15 = (bf16[128,1152]{1,0:T(8,128)(2,1)S(1)}, bf16[128,1152]{1,0:T(8,128)(2,1)S(1)}, u32[]{:S(2)}, u32[]{:S(2)}) collective-permute-start(bf16[128,1152]{1,0:T(8,128)(2,1)S(1)} %collective-permute-done.13.refs_2_), channel_id=1, source_target_pairs={{0,62},{1,3},{2,0},{3,5},{4,2},{5,7},{6,4},{7,9},{8,6},{9,11},{10,... | collective-permute-start | bytes 884744 | tf_op jit(solution)/shard_map/ppermute | solution.py:258
  81.3 10.4 %collective-permute-start.14 = (bf16[128,1152]{1,0:T(8,128)(2,1)S(1)}, bf16[128,1152]{1,0:T(8,128)(2,1)S(1)}, u32[]{:S(2)}, u32[]{:S(2)}) collective-permute-start(bf16[128,1152]{1,0:T(8,128)(2,1)S(1)} %collective-permute-done.10.refs_0_), channel_id=1, source_target_pairs={{0,2},{1,63},{2,4},{3,1},{4,6},{5,3},{6,8},{7,5},{8,10},{9,7},{10,... | collective-permute-start | bytes 884744 | tf_op jit(solution)/shard_map/ppermute | solution.py:258

commit v2 on v1

--- a/solution.py
+++ b/solution.py
@@ -102,10 +102,9 @@
         sums[rows, :] = old[rows, :] + against(scalars, unit[rows, :], scratch[...])
 
 
-def project(scalars, own, sums, first, outs, semaphores):
-    rows = own.shape[0]
-    step = 128
-    for a in range(0, rows, step):
+def project(scalars, own, sums, first, outs, semaphores, begin):
+    step = TILE // 2
+    for a in range(begin, begin + TILE, step):
         piece = pl.ds(a, step)
         units, inverse = normalized(own[piece, :])
         gradient = scalars[0:1, 0:1] * sums[piece, :]
@@ -125,20 +124,22 @@
         def _():
             copy(1).start()
 
-    for a in range(0, rows, step):
-        piece = pl.ds(a, step)
-        pltpu.make_async_copy(
-            sums.at[piece, :], outs[0].at[piece, :], semaphores.at[a // step]
-        ).wait()
-
 
 def last_kernel(n, side, scalars, own, unit, old, *refs):
     out0, out1, scratch, total, semaphores = refs[-5:]
     fill(scratch, refs[:n])
-    for rows in tiles(unit.shape[0]):
+    flag = jnp.max(scalars[2:3, :])
+    first = flag > 0.5 if side == 1 else flag < 0.5
+    for a in range(0, unit.shape[0], TILE):
+        rows = pl.ds(a, TILE)
         total[rows, :] = old[rows, :] + against(scalars, unit[rows, :], scratch[...])
-    first = jnp.max(scalars[2:3, :]) > 0.5 if side == 1 else jnp.max(scalars[2:3, :]) < 0.5
-    project(scalars, own, total, first, (out0, out1), semaphores)
+        project(scalars, own, total, first, (out0, out1), semaphores, a)
+    step = TILE // 2
+    for a in range(0, unit.shape[0], step):
+        piece = pl.ds(a, step)
+        pltpu.make_async_copy(
+            total.at[piece, :], out0.at[piece, :], semaphores.at[a // step]
+        ).wait()
 
 
 VMEM = pl.BlockSpec(memory_space=pltpu.VMEM)

time: 95.7 us -> 95.4 us (level)
  transfers between devices with their start and end apart: 16 -> 16, of which waited for: 5 -> 5; matrix products, arithmetic and copies ran while one was open for 4% -> 4% of each run, Pallas kernels for 31% -> 30%
where the time goes in v2:
time: 95.4 us; the launch traced here: 95.1 us
  starting transfers between devices  41.2 us (43%)
  Pallas kernels  32.2 us (34%)
  waiting for transfers between devices  13.2 us (14%)
  other arithmetic  6.25 us (7%)
  between operations  2.35 us (2%)
    ppermute x16, starting transfers between devices, shards(): there[n] = lax.ppermute(value, 'blk', routes[n[0]])  41.2 us
    pallas_call x8, Pallas kernels, call(): pl.pallas_call(kernel, in_specs=specs, out_specs=out_specs, out_shape=out...  32.2 us
    ppermute x16, waiting for transfers between devices, shards(): there[n] = lax.ppermute(value, 'blk', routes[n[0]])  13.2 us
    select_n x3, other arithmetic, one(): return jnp.where(even, caption[a:b], visual[a:b])  3.7 us
    select_n x1, other arithmetic, two(): return jnp.where(even, visual[a:b], caption[a:b])  2.47 us
  transfers between devices with their start and end apart: 16, of which 5 were waited for; matrix products, arithmetic and copies ran while one was open for 4% of the time, Pallas kernels for 30%

profile of v2, /device:TPU:2, one launch (start us, length us, event | category | flops | bytes accessed | tf_op | source)
XLA Modules:
  0.0 95.1 jit_solution(4700295632181457088)
XLA Ops:
  0.6 0.0 copy-start
  0.7 2.5 %broadcast_select_fusion.4 = (bf16[256,1152]{1,0:T(8,128)(2,1)}, bf16[256,1152]{1,0:T(8,128)(2,1)}) fusion(pred[]{:T(512)S(6)} %eq.23, bf16[640,1152]{1,0:T(8,128)(2,1)} %param.4, bf16[640,1152]{1,0:T(8,128)(2,1)} %param.5), kind=kLoop, calls=%fused_computation.4 | loop fusion | flops 589824 | bytes 2359297 | tf_op jit(solution)/shard_map/jit(_where)/select_n | solution.py:182
  3.1 2.1 %collective-permute-start.2 = (bf16[256,1152]{1,0:T(8,128)(2,1)}, bf16[256,1152]{1,0:T(8,128)(2,1)}, u32[]{:S(2)}, u32[]{:S(2)}) collective-permute-start(bf16[256,1152]{1,0:T(8,128)(2,1)} %get-tuple-element.47), channel_id=1, source_target_pairs={{0,1},{1,0},{2,3},{3,2},{4,5},{5,4},{6,7},{7,6},{8,9},{9,8},{10,11... | collective-permute-start | bytes 1769480 | tf_op jit(solution)/shard_map/ppermute | solution.py:259
  5.3 8.3 %collective-permute-start.1 = (bf16[256,1152]{1,0:T(8,128)(2,1)}, bf16[256,1152]{1,0:T(8,128)(2,1)}, u32[]{:S(2)}, u32[]{:S(2)}) collective-permute-start(bf16[256,1152]{1,0:T(8,128)(2,1)} %get-tuple-element.46), channel_id=1, source_target_pairs={{0,62},{1,3},{2,0},{3,5},{4,2},{5,7},{6,4},{7,9},{8,6},{9,11},{10,... | collective-permute-start | bytes 1769480 | tf_op jit(solution)/shard_map/ppermute | solution.py:259
  13.6 0.0 copy-done
  13.6 1.7 %broadcast_select_fusion = (bf16[640,1152]{1,0:T(8,128)(2,1)S(1)}, bf16[640,1152]{1,0:T(8,128)(2,1)S(1)}) fusion(bf16[640,1152]{1,0:T(8,128)(2,1)S(1)} %copy-done, bf16[640,1152]{1,0:T(8,128)(2,1)} %param.4, pred[]{:T(512)S(6)} %eq.23), kind=kLoop, calls=%fused_computation | loop fusion | flops 1474560 | bytes 5898241 | tf_op jit(solution)/shard_map/jit(_where)/select_n | solution.py:179
  15.2 0.1 collective-permute-start
  15.3 0.0 copy-done.1
  15.3 1.1 %broadcast_select_fusion.2 = (bf16[256,1152]{1,0:T(8,128)(2,1)}, bf16[256,1152]{1,0:T(8,128)(2,1)}) fusion(pred[]{:T(512)S(6)} %eq.23, bf16[640,1152]{1,0:T(8,128)(2,1)S(1)} %copy-done, bf16[640,1152]{1,0:T(8,128)(2,1)S(1)} %copy-done.1), kind=kLoop, calls=%fused_computation.2 | loop fusion | flops 589824 | bytes 2359297 | tf_op jit(solution)/shard_map/jit(_where)/select_n | solution.py:179
  16.5 1.5 %collective-permute-start.5 = (bf16[256,1152]{1,0:T(8,128)(2,1)}, bf16[256,1152]{1,0:T(8,128)(2,1)S(1)}, u32[]{:S(2)}, u32[]{:S(2)}) collective-permute-start(bf16[256,1152]{1,0:T(8,128)(2,1)} %get-tuple-element.42), channel_id=1, source_target_pairs={{0,1},{1,0},{2,3},{3,2},{4,5},{5,4},{6,7},{7,6},{8,9},{9,8},{10,11... | collective-permute-start | bytes 1769480 | tf_op jit(solution)/shard_map/ppermute | solution.py:259
  18.0 3.8 %collective-permute-start.4 = (bf16[256,1152]{1,0:T(8,128)(2,1)}, bf16[256,1152]{1,0:T(8,128)(2,1)}, u32[]{:S(2)}, u32[]{:S(2)}) collective-permute-start(bf16[256,1152]{1,0:T(8,128)(2,1)} %get-tuple-element.43), channel_id=1, source_target_pairs={{0,62},{1,3},{2,0},{3,5},{4,2},{5,7},{6,4},{7,9},{8,6},{9,11},{10,... | collective-permute-start | bytes 1769480 | tf_op jit(solution)/shard_map/ppermute | solution.py:259
  21.8 0.9 broadcast_select_fusion.6
  24.0 0.1 broadcast_select_fusion.8.scalars
  24.1 5.0 %shard_map.59 = (bf16[640,1152]{1,0:T(8,128)(2,1)S(1)}, bf16[640,1152]{1,0:T(8,128)(2,1)S(1)}, f32[640,1152]{1,0:T(8,128)S(1)}, f32[640,1152]{1,0:T(8,128)S(1)}) custom-call(f32[8,128]{1,0:T(8,128)S(1)} %broadcast_select_fusion.8.scalars, bf16[640,1152]{1,0:T(8,128)(2,1)S(1)} %get-tuple-element.44.own1.own, bf16[640,1152]{1,0:T(8,128)(2,1)S(1)} %get-tuple-element.45.own2.own), custom_call_target="tpu_custom_call" | custom-call | flops 3774873600 | bytes 1048576 | tf_op jit(solution)/shard_map/pallas_call | solution.py:151
  29.1 0.0 collective-permute-done.2.refs_3_
  29.1 0.0 collective-permute-done.1.refs_0_
  29.2 4.3 %collective-permute-start.7 = (bf16[128,1152]{1,0:T(8,128)(2,1)S(1)}, bf16[128,1152]{1,0:T(8,128)(2,1)S(1)}, u32[]{:S(2)}, u32[]{:S(2)}) collective-permute-start(bf16[128,1152]{1,0:T(8,128)(2,1)S(1)} %copy-done.3), channel_id=1, source_target_pairs={{0,62},{1,3},{2,0},{3,5},{4,2},{5,7},{6,4},{7,9},{8,6},{9,11},{10,... | collective-permute-start | bytes 884744 | tf_op jit(solution)/shard_map/ppermute | solution.py:259
  33.5 0.0 collective-permute-start.3
  33.5 0.0 collective-permute-done.5.refs_4_
  33.5 6.8 %collective-permute-done.4.refs_1_ = bf16[256,1152]{1,0:T(8,128)(2,1)} collective-permute-done((bf16[256,1152]{1,0:T(8,128)(2,1)}, bf16[256,1152]{1,0:T(8,128)(2,1)}, u32[]{:S(2)}, u32[]{:S(2)}) %collective-permute-start.4) | collective-permute-done | bytes 589856 | tf_op jit(solution)/shard_map/ppermute | solution.py:259
  40.3 5.8 %collective-permute-start.9 = (bf16[256,1152]{1,0:T(8,128)(2,1)}, bf16[256,1152]{1,0:T(8,128)(2,1)S(1)}, u32[]{:S(2)}, u32[]{:S(2)}) collective-permute-start(bf16[256,1152]{1,0:T(8,128)(2,1)} %collective-permute-done.2.refs_3_), channel_id=1, source_target_pairs={{0,62},{1,3},{2,0},{3,5},{4,2},{5,7},{6,4},{7,9},{8,6},{9,11},{10,... | collective-permute-start | bytes 1769480 | tf_op jit(solution)/shard_map/ppermute | solution.py:259
  46.1 0.0 collective-permute-start.6
  46.1 0.3 collective-permute-done.7.refs_2_
  46.4 6.6 %shard_map.61.old = f32[640,1152]{1,0:T(8,128)S(1)} custom-call(f32[8,128]{1,0:T(8,128)S(1)} %broadcast_select_fusion.8.scalars, bf16[640,1152]{1,0:T(8,128)(2,1)S(1)} %get-tuple-element.28.unit, f32[640,1152]{1,0:T(8,128)S(1)} %get-tuple-element.25.old, bf16[256,1152]{1,0:T(8,128)(2,1)} %collective-permute-done.1.refs_0_, ...), custom_call_target="tpu_custom_call", output_to_operand_aliasing={{}: (2, {})} | custom-call | flops 3397386240 | bytes 1048576 | tf_op jit(solution)/shard_map/pallas_call | solution.py:151
  53.0 0.0 collective-permute-done.3.refs_1_
  53.0 0.1 collective-permute-start.8
  53.1 0.0 collective-permute-done.refs_0_
  53.1 5.9 %collective-permute-start.12 = (bf16[256,1152]{1,0:T(8,128)(2,1)S(1)}, bf16[256,1152]{1,0:T(8,128)(2,1)S(1)}, u32[]{:S(2)}, u32[]{:S(2)}) collective-permute-start(bf16[256,1152]{1,0:T(8,128)(2,1)S(1)} %collective-permute-done.5.refs_4_), channel_id=1, source_target_pairs={{0,62},{1,3},{2,0},{3,5},{4,2},{5,7},{6,4},{7,9},{8,6},{9,11},{10,... | collective-permute-start | bytes 1769480 | tf_op jit(solution)/shard_map/ppermute | solution.py:259
  59.0 0.0 collective-permute-start.13
  59.0 5.5 %shard_map.60.old = f32[640,1152]{1,0:T(8,128)S(1)} custom-call(f32[8,128]{1,0:T(8,128)S(1)} %broadcast_select_fusion.8.scalars, bf16[640,1152]{1,0:T(8,128)(2,1)S(1)} %get-tuple-element.23.unit, f32[640,1152]{1,0:T(8,128)S(1)} %get-tuple-element.24.old, bf16[640,1152]{1,0:T(8,128)(2,1)} %collective-permute-done.refs_0_, ...), custom_call_target="tpu_custom_call", output_to_operand_aliasing={{}: (2, {})} | custom-call | flops 2642411520 | bytes 1048576 | tf_op jit(solution)/shard_map/pallas_call | solution.py:151
  64.5 0.0 collective-permute-done.9.refs_0_
  64.5 0.0 collective-permute-done.6.refs_0_
  64.6 0.1 collective-permute-start.11
  64.7 5.4 %collective-permute-start.10 = (bf16[128,1152]{1,0:T(8,128)(2,1)S(1)}, bf16[128,1152]{1,0:T(8,128)(2,1)S(1)}, u32[]{:S(2)}, u32[]{:S(2)}) collective-permute-start(bf16[128,1152]{1,0:T(8,128)(2,1)S(1)} %collective-permute-done.7.refs_2_), channel_id=1, source_target_pairs={{0,1},{1,0},{2,3},{3,2},{4,5},{5,4},{6,7},{7,6},{8,9},{9,8},{10,11... | collective-permute-start | bytes 884744 | tf_op jit(solution)/shard_map/ppermute | solution.py:259
  70.1 1.6 %collective-permute-done.8.refs_1_ = bf16[256,1152]{1,0:T(8,128)(2,1)S(1)} collective-permute-done((bf16[256,1152]{1,0:T(8,128)(2,1)S(1)}, bf16[256,1152]{1,0:T(8,128)(2,1)S(1)}, u32[]{:S(2)}, u32[]{:S(2)}) %collective-permute-start.8) | collective-permute-done | bytes 589856 | tf_op jit(solution)/shard_map/ppermute | solution.py:259
  71.7 2.6 %shard_map.62.old = f32[640,1152]{1,0:T(8,128)S(1)} custom-call(f32[8,128]{1,0:T(8,128)S(1)} %broadcast_select_fusion.8.scalars, bf16[640,1152]{1,0:T(8,128)(2,1)S(1)} %get-tuple-element.23.unit, f32[640,1152]{1,0:T(8,128)S(1)} %shard_map.60.old, bf16[256,1152]{1,0:T(8,128)(2,1)S(1)} %collective-permute-done.6.refs_0_, ...), custom_call_target="tpu_custom_call", output_to_operand_aliasing={{}: (2, {})} | custom-call | flops 1509949440 | bytes 1048576 | tf_op jit(solution)/shard_map/pallas_call | solution.py:151
  74.3 0.0 collective-permute-done.13.refs_2_
  74.3 3.4 %collective-permute-start.15 = (bf16[128,1152]{1,0:T(8,128)(2,1)S(1)}, bf16[128,1152]{1,0:T(8,128)(2,1)S(1)}, u32[]{:S(2)}, u32[]{:S(2)}) collective-permute-start(bf16[128,1152]{1,0:T(8,128)(2,1)S(1)} %collective-permute-done.13.refs_2_), channel_id=1, source_target_pairs={{0,62},{1,3},{2,0},{3,5},{4,2},{5,7},{6,4},{7,9},{8,6},{9,11},{10,... | collective-permute-start | bytes 884744 | tf_op jit(solution)/shard_map/ppermute | solution.py:259
  77.7 0.0 collective-permute-done.12.refs_1_
  77.7 3.5 %shard_map.64.old = f32[640,1152]{1,0:T(8,128)S(1)} custom-call(f32[8,128]{1,0:T(8,128)S(1)} %broadcast_select_fusion.8.scalars, bf16[640,1152]{1,0:T(8,128)(2,1)S(1)} %get-tuple-element.28.unit, f32[640,1152]{1,0:T(8,128)S(1)} %shard_map.61.old, bf16[256,1152]{1,0:T(8,128)(2,1)S(1)} %collective-permute-done.9.refs_0_, ...), custom_call_target="tpu_custom_call", output_to_operand_aliasing={{}: (2, {})} | custom-call | flops 1887436800 | bytes 1048576 | tf_op jit(solution)/shard_map/pallas_call | solution.py:151
  81.3 0.0 collective-permute-done.10.refs_0_
  81.3 0.3 collective-permute-start.14
  81.6 0.4 collective-permute-done.15.refs_0_
  82.0 3.3 %shard_map.65 = (f32[640,1152]{1,0:T(8,128)}, f32[640,1152]{1,0:T(8,128)}) custom-call(f32[8,128]{1,0:T(8,128)S(1)} %broadcast_select_fusion.8.scalars, bf16[640,1152]{1,0:T(8,128)(2,1)S(1)} %get-tuple-element.44.own1.own, bf16[640,1152]{1,0:T(8,128)(2,1)S(1)} %get-tuple-element.28.unit, f32[640,1152]{1,0:T(8,128)S(1)} %shard_map.64.old, ...), custom_call_target="tpu_custom_call" | custom-call | flops 377487360 | bytes 1048576 | tf_op jit(solution)/shard_map/pallas_call | solution.py:151
  85.3 0.0 collective-permute-done.11.refs_1_
  85.3 2.4 %shard_map.63.old = f32[640,1152]{1,0:T(8,128)S(1)} custom-call(f32[8,128]{1,0:T(8,128)S(1)} %broadcast_select_fusion.8.scalars, bf16[640,1152]{1,0:T(8,128)(2,1)S(1)} %get-tuple-element.23.unit, f32[640,1152]{1,0:T(8,128)S(1)} %shard_map.62.old, bf16[128,1152]{1,0:T(8,128)(2,1)S(1)} %collective-permute-done.10.refs_0_, ...), custom_call_target="tpu_custom_call", output_to_operand_aliasing={{}: (2, {})} | custom-call | flops 1132462080 | bytes 1048576 | tf_op jit(solution)/shard_map/pallas_call | solution.py:151
  87.7 4.0 %collective-permute-done.14.refs_0_ = bf16[128,1152]{1,0:T(8,128)(2,1)S(1)} collective-permute-done((bf16[128,1152]{1,0:T(8,128)(2,1)S(1)}, bf16[128,1152]{1,0:T(8,128)(2,1)S(1)}, u32[]{:S(2)}, u32[]{:S(2)}) %collective-permute-start.14) | collective-permute-done | bytes 294944 | tf_op jit(solution)/shard_map/ppermute | solution.py:259
  91.6 3.3 %shard_map.66 = (f32[640,1152]{1,0:T(8,128)}, f32[640,1152]{1,0:T(8,128)}) custom-call(f32[8,128]{1,0:T(8,128)S(1)} %broadcast_select_fusion.8.scalars, bf16[640,1152]{1,0:T(8,128)(2,1)S(1)} %get-tuple-element.45.own2.own, bf16[640,1152]{1,0:T(8,128)(2,1)S(1)} %get-tuple-element.23.unit, ...), custom_call_target="tpu_custom_call", output_to_operand_aliasing={{0}: (5, {}), {1}: (6, {})} | custom-call | flops 377487360 | bytes 1048576 | tf_op jit(solution)/shard_map/pallas_call | solution.py:151
  (7 shorter events, 0.0 us)
Async XLA Ops:
  0.6 12.9 %copy-start = (bf16[640,1152]{1,0:T(8,128)(2,1)S(1)}, bf16[640,1152]{1,0:T(8,128)(2,1)}, u32[]{:S(2)}) copy-start(bf16[640,1152]{1,0:T(8,128)(2,1)} %param.5) | copy-start | bytes 4423684
  3.1 26.0 %collective-permute-start.2 = (bf16[256,1152]{1,0:T(8,128)(2,1)}, bf16[256,1152]{1,0:T(8,128)(2,1)}, u32[]{:S(2)}, u32[]{:S(2)}) collective-permute-start(bf16[256,1152]{1,0:T(8,128)(2,1)} %get-tuple-element.47), channel_id=1, source_target_pairs={{0,1},{1,0},{2,3},{3,2},{4,5},{5,4},{6,7},{7,6},{8,9},{9,8},{10,11... | collective-permute-start | bytes 1769480 | tf_op jit(solution)/shard_map/ppermute | solution.py:259
  5.3 10.1 %copy-start.1 = (bf16[640,1152]{1,0:T(8,128)(2,1)S(1)}, bf16[640,1152]{1,0:T(8,128)(2,1)}, u32[]{:S(2)}) copy-start(bf16[640,1152]{1,0:T(8,128)(2,1)} %param.4) | copy-start | bytes 4423684
  5.3 23.9 %collective-permute-start.1 = (bf16[256,1152]{1,0:T(8,128)(2,1)}, bf16[256,1152]{1,0:T(8,128)(2,1)}, u32[]{:S(2)}, u32[]{:S(2)}) collective-permute-start(bf16[256,1152]{1,0:T(8,128)(2,1)} %get-tuple-element.46), channel_id=1, source_target_pairs={{0,62},{1,3},{2,0},{3,5},{4,2},{5,7},{6,4},{7,9},{8,6},{9,11},{10,... | collective-permute-start | bytes 1769480 | tf_op jit(solution)/shard_map/ppermute | solution.py:259
  15.2 37.9 %collective-permute-start = (bf16[640,1152]{1,0:T(8,128)(2,1)S(1)}, bf16[640,1152]{1,0:T(8,128)(2,1)}, u32[]{:S(2)}, u32[]{:S(2)}) collective-permute-start(bf16[640,1152]{1,0:T(8,128)(2,1)S(1)} %get-tuple-element.44.own1.own), channel_id=1, source_target_pairs={{0,2},{1,63},{2,4},{3,1},{4,6},{5,3},{6,8},{7,5},{8,10},{9,7},{10,... | collective-permute-start | bytes 4423688 | tf_op jit(solution)/shard_map/ppermute | solution.py:259
  16.5 17.0 %collective-permute-start.5 = (bf16[256,1152]{1,0:T(8,128)(2,1)}, bf16[256,1152]{1,0:T(8,128)(2,1)S(1)}, u32[]{:S(2)}, u32[]{:S(2)}) collective-permute-start(bf16[256,1152]{1,0:T(8,128)(2,1)} %get-tuple-element.42), channel_id=1, source_target_pairs={{0,1},{1,0},{2,3},{3,2},{4,5},{5,4},{6,7},{7,6},{8,9},{9,8},{10,11... | collective-permute-start | bytes 1769480 | tf_op jit(solution)/shard_map/ppermute | solution.py:259
  18.0 22.3 %collective-permute-start.4 = (bf16[256,1152]{1,0:T(8,128)(2,1)}, bf16[256,1152]{1,0:T(8,128)(2,1)}, u32[]{:S(2)}, u32[]{:S(2)}) collective-permute-start(bf16[256,1152]{1,0:T(8,128)(2,1)} %get-tuple-element.43), channel_id=1, source_target_pairs={{0,62},{1,3},{2,0},{3,5},{4,2},{5,7},{6,4},{7,9},{8,6},{9,11},{10,... | collective-permute-start | bytes 1769480 | tf_op jit(solution)/shard_map/ppermute | solution.py:259
  24.1 5.1 %copy-start.3 = (bf16[128,1152]{1,0:T(8,128)(2,1)S(1)}, bf16[128,1152]{1,0:T(8,128)(2,1)}, u32[]{:S(2)}) copy-start(bf16[128,1152]{1,0:T(8,128)(2,1)} %get-tuple-element.29) | copy-start | bytes 884740
  29.2 17.3 %collective-permute-start.7 = (bf16[128,1152]{1,0:T(8,128)(2,1)S(1)}, bf16[128,1152]{1,0:T(8,128)(2,1)S(1)}, u32[]{:S(2)}, u32[]{:S(2)}) collective-permute-start(bf16[128,1152]{1,0:T(8,128)(2,1)S(1)} %copy-done.3), channel_id=1, source_target_pairs={{0,62},{1,3},{2,0},{3,5},{4,2},{5,7},{6,4},{7,9},{8,6},{9,11},{10,... | collective-permute-start | bytes 884744 | tf_op jit(solution)/shard_map/ppermute | solution.py:259
  33.5 19.6 %collective-permute-start.3 = (bf16[256,1152]{1,0:T(8,128)(2,1)}, bf16[256,1152]{1,0:T(8,128)(2,1)S(1)}, u32[]{:S(2)}, u32[]{:S(2)}) collective-permute-start(bf16[256,1152]{1,0:T(8,128)(2,1)} %collective-permute-done.1.refs_0_), channel_id=1, source_target_pairs={{0,1},{1,0},{2,3},{3,2},{4,5},{5,4},{6,7},{7,6},{8,9},{9,8},{10,11... | collective-permute-start | bytes 1769480 | tf_op jit(solution)/shard_map/ppermute | solution.py:259
  40.3 24.3 %collective-permute-start.9 = (bf16[256,1152]{1,0:T(8,128)(2,1)}, bf16[256,1152]{1,0:T(8,128)(2,1)S(1)}, u32[]{:S(2)}, u32[]{:S(2)}) collective-permute-start(bf16[256,1152]{1,0:T(8,128)(2,1)} %collective-permute-done.2.refs_3_), channel_id=1, source_target_pairs={{0,62},{1,3},{2,0},{3,5},{4,2},{5,7},{6,4},{7,9},{8,6},{9,11},{10,... | collective-permute-start | bytes 1769480 | tf_op jit(solution)/shard_map/ppermute | solution.py:259
  46.1 18.5 %collective-permute-start.6 = (bf16[256,1152]{1,0:T(8,128)(2,1)}, bf16[256,1152]{1,0:T(8,128)(2,1)S(1)}, u32[]{:S(2)}, u32[]{:S(2)}) collective-permute-start(bf16[256,1152]{1,0:T(8,128)(2,1)} %collective-permute-done.4.refs_1_), channel_id=1, source_target_pairs={{0,1},{1,0},{2,3},{3,2},{4,5},{5,4},{6,7},{7,6},{8,9},{9,8},{10,11... | collective-permute-start | bytes 1769480 | tf_op jit(solution)/shard_map/ppermute | solution.py:259
  46.4 12.6 %copy-start.2 = (bf16[128,1152]{1,0:T(8,128)(2,1)S(1)}, bf16[128,1152]{1,0:T(8,128)(2,1)}, u32[]{:S(2)}) copy-start(bf16[128,1152]{1,0:T(8,128)(2,1)} %get-tuple-element.35) | copy-start | bytes 884740
  53.0 18.7 %collective-permute-start.8 = (bf16[256,1152]{1,0:T(8,128)(2,1)S(1)}, bf16[256,1152]{1,0:T(8,128)(2,1)S(1)}, u32[]{:S(2)}, u32[]{:S(2)}) collective-permute-start(bf16[256,1152]{1,0:T(8,128)(2,1)S(1)} %collective-permute-done.3.refs_1_), channel_id=1, source_target_pairs={{0,2},{1,63},{2,4},{3,1},{4,6},{5,3},{6,8},{7,5},{8,10},{9,7},{10,... | collective-permute-start | bytes 1769480 | tf_op jit(solution)/shard_map/ppermute | solution.py:259
  53.1 24.6 %collective-permute-start.12 = (bf16[256,1152]{1,0:T(8,128)(2,1)S(1)}, bf16[256,1152]{1,0:T(8,128)(2,1)S(1)}, u32[]{:S(2)}, u32[]{:S(2)}) collective-permute-start(bf16[256,1152]{1,0:T(8,128)(2,1)S(1)} %collective-permute-done.5.refs_4_), channel_id=1, source_target_pairs={{0,62},{1,3},{2,0},{3,5},{4,2},{5,7},{6,4},{7,9},{8,6},{9,11},{10,... | collective-permute-start | bytes 1769480 | tf_op jit(solution)/shard_map/ppermute | solution.py:259
  59.0 15.3 %collective-permute-start.13 = (bf16[128,1152]{1,0:T(8,128)(2,1)S(1)}, bf16[128,1152]{1,0:T(8,128)(2,1)S(1)}, u32[]{:S(2)}, u32[]{:S(2)}) collective-permute-start(bf16[128,1152]{1,0:T(8,128)(2,1)S(1)} %copy-done.2), channel_id=1, source_target_pairs={{0,1},{1,0},{2,3},{3,2},{4,5},{5,4},{6,7},{7,6},{8,9},{9,8},{10,11... | collective-permute-start | bytes 884744 | tf_op jit(solution)/shard_map/ppermute | solution.py:259
  64.6 20.7 %collective-permute-start.11 = (bf16[256,1152]{1,0:T(8,128)(2,1)S(1)}, bf16[256,1152]{1,0:T(8,128)(2,1)S(1)}, u32[]{:S(2)}, u32[]{:S(2)}) collective-permute-start(bf16[256,1152]{1,0:T(8,128)(2,1)S(1)} %collective-permute-done.6.refs_0_), channel_id=1, source_target_pairs={{0,2},{1,63},{2,4},{3,1},{4,6},{5,3},{6,8},{7,5},{8,10},{9,7},{10,... | collective-permute-start | bytes 1769480 | tf_op jit(solution)/shard_map/ppermute | solution.py:259
  64.7 16.6 %collective-permute-start.10 = (bf16[128,1152]{1,0:T(8,128)(2,1)S(1)}, bf16[128,1152]{1,0:T(8,128)(2,1)S(1)}, u32[]{:S(2)}, u32[]{:S(2)}) collective-permute-start(bf16[128,1152]{1,0:T(8,128)(2,1)S(1)} %collective-permute-done.7.refs_2_), channel_id=1, source_target_pairs={{0,1},{1,0},{2,3},{3,2},{4,5},{5,4},{6,7},{7,6},{8,9},{9,8},{10,11... | collective-permute-start | bytes 884744 | tf_op jit(solution)/shard_map/ppermute | solution.py:259
  74.3 7.6 %collective-permute-start.15 = (bf16[128,1152]{1,0:T(8,128)(2,1)S(1)}, bf16[128,1152]{1,0:T(8,128)(2,1)S(1)}, u32[]{:S(2)}, u32[]{:S(2)}) collective-permute-start(bf16[128,1152]{1,0:T(8,128)(2,1)S(1)} %collective-permute-done.13.refs_2_), channel_id=1, source_target_pairs={{0,62},{1,3},{2,0},{3,5},{4,2},{5,7},{6,4},{7,9},{8,6},{9,11},{10,... | collective-permute-start | bytes 884744 | tf_op jit(solution)/shard_map/ppermute | solution.py:259
  81.3 10.4 %collective-permute-start.14 = (bf16[128,1152]{1,0:T(8,128)(2,1)S(1)}, bf16[128,1152]{1,0:T(8,128)(2,1)S(1)}, u32[]{:S(2)}, u32[]{:S(2)}) collective-permute-start(bf16[128,1152]{1,0:T(8,128)(2,1)S(1)} %collective-permute-done.10.refs_0_), channel_id=1, source_target_pairs={{0,2},{1,63},{2,4},{3,1},{4,6},{5,3},{6,8},{7,5},{8,10},{9,7},{10,... | collective-permute-start | bytes 884744 | tf_op jit(solution)/shard_map/ppermute | solution.py:259
